TPU v7x, 32 devices: a whole 2x2x4 slice. The times are simulated.
32 devices in a mesh: wide: 8 (over y, x, core), layer: 4 (over z).
Axes of the slice: x: 2, y: 2, z: 4, core: 2. Of those that a mesh axis runs over, the one named last changes fastest.
Arguments:
- factor: float32 [4096, 1024], P('layer', 'wide'), parts along dimension 0, may hold values from -1 to 21, as said below
Outputs:
- rotated: float32 [4096, 1024], P('layer', 'wide'), parts along dimension 0
- eigen_basis: float32 [4096, 1024], P('layer', 'wide'), parts along dimension 0
There are 4 independent parts, one for each index of `layer`. A program takes and returns all parts, laid end to end along the dimension named above; each array names one. Nothing has to cross between parts.
Inputs may be any that keep to these rules, and one draw needn't show every extreme that they name: `factor`: symmetric.
All inputs are finite; a program needn't handle non-finite values.
Results may differ from a plain program's by a relative error of at most 0.00095.
Values sent between devices are 32-bit elements; how exact they have to be, the bound alone decides.
No kernel may reach another device: no remote copies, remote signals or barrier semaphores. Data moves between devices by JAX's collectives and lax.ppermute only.
A program may use at most 128 MiB of HBM per device.

v0:
```python
import functools
import jax
import jax.numpy as jnp
from jax import lax
from jax.experimental import pallas as pl
from jax.experimental.pallas import tpu as pltpu
from jax.sharding import PartitionSpec as P

SWEEPS = 3
FLOOR = 0.01
TOLERANCE = 2e-6


def schedule(bound, steps=None, goal=1e-6):
    theta = bound / (2.0 + bound)
    mus = []
    while len(mus) < steps if steps else theta > goal:
        mus.append(2.0 / (2.0 - theta * theta))
        theta = theta * theta / (2.0 - theta * theta)
    return 1.0 / (1.0 + 0.5 * bound), tuple(mus)


def split(x):
    high = x.astype(jnp.bfloat16)
    x = x - high.astype(jnp.float32)
    middle = x.astype(jnp.bfloat16)
    return high, middle, (x - middle.astype(jnp.float32)).astype(jnp.bfloat16)


def product(a, b):
    n = b.shape[1]
    a_high, a_middle, a_low = split(a)
    b_high, b_middle, b_low = split(b)
    wide = jnp.concatenate([b_high, b_middle], axis=1)
    most = jnp.dot(
        jnp.concatenate([a_high, a_middle], axis=1),
        jnp.concatenate([wide, wide], axis=0),
        preferred_element_type=jnp.float32,
    )
    rest = jnp.dot(
        jnp.concatenate([a_high, a_low], axis=1),
        jnp.concatenate([b_low, b_high], axis=0),
        preferred_element_type=jnp.float32,
    )
    return most[:, :n] + (most[:, n:] + rest)


def exact(a, b):
    return jnp.dot(a, b, precision=lax.Precision.HIGHEST, preferred_element_type=jnp.float32)


def identity_of(n):
    row = lax.broadcasted_iota(jnp.int32, (n, n), 0)
    col = lax.broadcasted_iota(jnp.int32, (n, n), 1)
    return (row == col).astype(jnp.float32)


def half_skew(m, eye):
    kept = m * eye
    spread = jnp.sum(kept, axis=0, keepdims=True) - jnp.sum(kept, axis=1, keepdims=True)
    ratios = m * spread / (spread * spread + 2.0 * m * m + FLOOR)
    return 0.25 * (ratios - ratios.T)


def sure_sweep(m, q, eye):
    n = m.shape[0]
    a = half_skew(m, eye)
    system = eye - exact(a, a)
    scale, mus = schedule(n * n / 32.0)

    def newton(_, y):
        return y + exact(y, eye - exact(system, y))

    y = lax.fori_loop(0, len(mus) + 6, newton, scale * eye)
    x = exact(y, eye + a)
    x = x + exact(x, eye - (x - exact(a, x)))
    turn = 2.0 * x - eye
    return exact(turn.T, exact(m, turn)), exact(q, turn)


def sweep(m, q, eye, plan):
    n = m.shape[0]
    scale, mus = plan
    a = half_skew(m, eye)
    rows = [a, m] if q is None else [a, m, q]
    first = product(jnp.concatenate(rows, axis=0), a)
    error = (1.0 - scale) * eye + scale * first[:n]
    left = scale * (eye - a)
    m_right = scale * (m + first[n : 2 * n])
    q_right = scale * (eye + a) if q is None else scale * (q + first[2 * n :])
    for mu in mus:
        step = product(jnp.concatenate([error, left, m_right, q_right], axis=0), error)
        error = (1.0 - mu) * eye + mu * step[:n]
        left = mu * (left + step[n : 2 * n])
        m_right = mu * (m_right + step[2 * n : 3 * n])
        q_right = mu * (q_right + step[3 * n :])
    q = 2.0 * q_right - (eye if q is None else q)
    m = product(2.0 * left - eye, 2.0 * m_right - m)
    return m, q, jnp.sum(error * error, axis=0, keepdims=True)


def solve(blocks, plans, eye):
    ms, qs = list(blocks), [None] * len(blocks)
    worst = jnp.zeros((1, eye.shape[0]), jnp.float32)
    for plan in plans:
        for k in range(len(ms)):
            ms[k], qs[k], left_over = sweep(ms[k], qs[k], eye, plan)
            worst = worst + left_over
    return ms, qs, worst


def solve_into(blocks, plans, m_ref, q_ref):
    n = blocks[0].shape[0]
    eye = identity_of(n)
    ms, qs, worst = solve(blocks, plans, eye)
    for k in range(len(ms)):
        m_ref[k] = ms[k]
        q_ref[k] = qs[k]
    settled = jnp.sum(worst) <= TOLERANCE * TOLERANCE * n

    @pl.when(jnp.logical_not(settled))
    def _():
        for k in range(len(blocks)):
            m_ref[k] = blocks[k]
            q_ref[k] = eye

        def again(step, carry):
            k = step // SWEEPS
            m_ref[k], q_ref[k] = sure_sweep(m_ref[k], q_ref[k], eye)
            return carry

        lax.fori_loop(0, SWEEPS * len(blocks), again, 0)


PLANS = ((schedule(4.0, 4),) * SWEEPS, (schedule(0.8, 3),) * SWEEPS)


def solve_kernel(plans, block_ref, q_ref, m_ref):
    solve_into([block_ref[0]], plans, m_ref, q_ref)


def cayley_sweeps(pair_block, plans):
    n = pair_block.shape[0]
    return pl.pallas_call(
        functools.partial(solve_kernel, plans),
        out_shape=jax.ShapeDtypeStruct((1, n, n), jnp.float32),
        scratch_shapes=[pltpu.VMEM((1, n, n), jnp.float32)],
        compiler_params=pltpu.CompilerParams(vmem_limit_bytes=32 * 1024 * 1024),
    )(pair_block[None])[0]


def from_partner(shard, axis, bit):
    return lax.ppermute(shard, axis, [(i, i ^ 1 << bit) for i in range(lax.axis_size(axis))])


def trade_rows(current, wide_count, width_half):
    order_size, pair_span = current.shape
    split_view = current.reshape(2, wide_count // 2, 2, width_half, pair_span)
    joined = jnp.concatenate([split_view[:, :, :1], split_view[::-1, :, 1:]], axis=2)
    return joined.reshape(order_size, pair_span)


def one_round(current, basis, my_pair, plans):
    order_size, pair_span = current.shape
    pair_block = lax.dynamic_slice_in_dim(current, my_pair * pair_span, pair_span, 0)
    rotate = cayley_sweeps(pair_block, plans)
    columns = jnp.dot(current, rotate, precision=lax.Precision.HIGHEST)
    pieces = lax.all_gather(rotate[None], "wide", axis=0, tiled=True)
    how_many = pieces.shape[0]
    row_slab = columns
    row_slab = row_slab.reshape(how_many, pair_span, pair_span)
    updated = jnp.einsum("nba,nbc->nac", pieces, row_slab, precision=lax.Precision.HIGHEST)
    current = lax.dynamic_update_slice_in_dim(
        columns, updated.reshape(how_many * pair_span, pair_span), jnp.int32(0) * pair_span, 0
    )
    basis = jnp.dot(basis, rotate, precision=lax.Precision.HIGHEST)
    return (current, basis)


def body(factor):
    wide_count = lax.axis_size("wide")
    my_pair = lax.axis_index("wide")
    order_size, pair_span = factor.shape
    width_half = pair_span // 2
    row_index = lax.broadcasted_iota(jnp.int32, (order_size, pair_span), 0)
    col_index = lax.broadcasted_iota(jnp.int32, (order_size, pair_span), 1) + my_pair * pair_span
    basis = (row_index == col_index).astype(jnp.float32)
    current = factor
    for repeat in range(2):
        if repeat == 1:
            moved_factor, moved_basis = from_partner(
                (current[:, width_half:], basis[:, width_half:]),
                "wide",
                wide_count.bit_length() - 2,
            )
            current = jnp.concatenate([current[:, :width_half], moved_factor], axis=1)
            basis = jnp.concatenate([basis[:, :width_half], moved_basis], axis=1)
            current = trade_rows(current, wide_count, width_half)
        current, basis = one_round(current, basis, my_pair, PLANS[repeat])
    return (current, basis)


def solution(mesh):
    return jax.shard_map(
        body,
        mesh=mesh,
        in_specs=(P("layer", "wide"),),
        out_specs=(P("layer", "wide"), P("layer", "wide")),
        check_vma=False,
    )
```

profile of v0, /device:TPU:0, one launch (start us, length us, event | category | flops | bytes accessed | tf_op | source)
XLA Modules:
  0.0 52.3 jit_solution(6192242737961415022)
XLA Ops:
  0.6 0.0 copy-start
  0.6 1.0 %copy-done = f32[1024,128]{1,0:T(8,128)S(1)} copy-done((f32[1024,128]{1,0:T(8,128)S(1)}, f32[1024,128]{1,0:T(8,128)}, u32[]{:S(2)}) %copy-start) | copy-done | bytes 524312
  1.7 4.2 %shard_map.30 = f32[1,128,128]{2,1,0:T(8,128)S(1)} custom-call(f32[1,128,128]{2,1,0:T(8,128)S(1)} %dynamic-slice_bitcast_fusion.1.block_ref), custom_call_target="tpu_custom_call" | custom-call | tf_op jit(solution)/shard_map/pallas_call | solution.py:144
  5.9 11.3 %all_gather.6 = f32[8,128,128]{2,1,0:T(8,128)S(1)} all-gather(f32[1,128,128]{2,1,0:T(8,128)S(1)} %shard_map.30), channel_id=1, replica_groups=mesh['wide'=8,'layer'=4] {'wide'}, dimensions={0}, use_global_device_ids=true | all-gather | bytes 589824 | tf_op jit(solution)/shard_map/all_gather | solution.py:168
  17.2 0.6 %convolution_bitcast_fusion = f32[1024,128]{0,1:T(8,128)S(1)} fusion(f32[1024,128]{1,0:T(8,128)S(1)} %copy-done, f32[1,128,128]{2,1,0:T(8,128)S(1)} %shard_map.30), kind=kOutput, calls=%fused_computation | convolution fusion | flops 201326592 | bytes 1114112 | tf_op jit(solution)/shard_map/dot_general | solution.py:167
  17.8 0.2 copy.11
  18.0 1.0 %fusion.15 = f32[8,128,128]{2,1,0:T(8,128)S(1)} fusion(f32[8,128,128]{2,1,0:T(8,128)S(1)} %all_gather.6, f32[8,128,128]{2,1,0:T(8,128)S(1)} %bitcast.33), kind=kOutput, calls=%fused_computation.22 | convolution fusion | flops 201326592 | bytes 1572864 | tf_op jit(solution)/shard_map/nba,nbc->nac/dot_general | solution.py:172
  19.1 0.2 fusion.14
  19.3 1.6 %collective-permute-start = (f32[1024,64]{1,0:T(8,128)S(1)}, f32[1024,64]{1,0:T(8,128)S(1)}, u32[]{:S(2)}, u32[]{:S(2)}) collective-permute-start(f32[1024,64]{1,0:T(8,128)S(1)} %get-tuple-element.7), channel_id=1, source_target_pairs={{0,16},{4,20},{8,24},{12,28},{16,0},{20,4},{24,8},{28,12},{1,17},{... | collective-permute-start | bytes 786440 | tf_op jit(solution)/shard_map/ppermute | solution.py:153
  20.9 0.4 fusion.4
  21.3 0.6 %collective-permute-start.1 = (f32[1024,64]{0,1:T(8,128)S(1)}, f32[1024,64]{0,1:T(8,128)S(1)}, u32[]{:S(2)}, u32[]{:S(2)}) collective-permute-start(f32[1024,64]{0,1:T(8,128)S(1)} %get-tuple-element.3), channel_id=1, source_target_pairs={{0,16},{4,20},{8,24},{12,28},{16,0},{20,4},{24,8},{28,12},{1,17},{... | collective-permute-start | bytes 786440 | tf_op jit(solution)/shard_map/ppermute | solution.py:153
  21.9 12.2 %collective-permute-done = f32[1024,64]{1,0:T(8,128)S(1)} collective-permute-done((f32[1024,64]{1,0:T(8,128)S(1)}, f32[1024,64]{1,0:T(8,128)S(1)}, u32[]{:S(2)}, u32[]{:S(2)}) %collective-permute-start) | collective-permute-done | bytes 262176 | tf_op jit(solution)/shard_map/ppermute | solution.py:153
  34.1 0.2 pad_maximum_fusion
  34.4 3.6 %shard_map.31 = f32[1,128,128]{2,1,0:T(8,128)S(1)} custom-call(f32[1,128,128]{2,1,0:T(8,128)S(1)} %dynamic-slice_bitcast_fusion.block_ref), custom_call_target="tpu_custom_call" | custom-call | tf_op jit(solution)/shard_map/pallas_call | solution.py:144
  38.1 10.1 %all_gather.7 = f32[8,128,128]{2,1,0:T(8,128)S(1)} all-gather(f32[1,128,128]{2,1,0:T(8,128)S(1)} %shard_map.31), channel_id=1, replica_groups=mesh['wide'=8,'layer'=4] {'wide'}, dimensions={0}, use_global_device_ids=true | all-gather | bytes 589824 | tf_op jit(solution)/shard_map/all_gather | solution.py:168
  48.1 0.6 %fusion.6 = f32[8,128,128]{2,1,0:T(8,128)S(1)} fusion(f32[8,128,128]{2,1,0:T(8,128)S(1)} %bitcast.31, f32[1,128,128]{2,1,0:T(8,128)S(1)} %shard_map.31), kind=kOutput, calls=%fused_computation.10 | convolution fusion | flops 201326592 | bytes 1114112 | tf_op jit(solution)/shard_map/dot_general | solution.py:167
  48.7 1.8 %fusion.16 = f32[8,128,128]{2,1,0:T(8,128)} fusion(f32[8,128,128]{2,1,0:T(8,128)S(1)} %all_gather.7, f32[8,128,128]{2,1,0:T(8,128)S(1)} %fusion.6), kind=kOutput, calls=%fused_computation.23 | convolution fusion | flops 201326592 | bytes 1572864 | tf_op jit(solution)/shard_map/nba,nbc->nac/dot_general | solution.py:172
  50.5 0.0 collective-permute-done.1
  50.5 1.8 %fusion = f32[1024,128]{1,0:T(8,128)} fusion(f32[1024,64]{0,1:T(8,128)S(1)} %collective-permute-done.1, f32[1024,64]{0,1:T(8,128)S(1)} %get-tuple-element.2, f32[1,128,128]{2,1,0:T(8,128)S(1)} %shard_map.31), kind=kOutput, calls=%fused_computation.3 | convolution fusion | flops 201457664 | bytes 1114112 | tf_op jit(solution)/shard_map/dot_general | solution.py:176
  (7 shorter events, 0.2 us)
Async XLA Ops:
  0.6 1.0 %copy-start = (f32[1024,128]{1,0:T(8,128)S(1)}, f32[1024,128]{1,0:T(8,128)}, u32[]{:S(2)}) copy-start(f32[1024,128]{1,0:T(8,128)} %param.1) | copy-start | bytes 1572868
  19.3 14.8 %collective-permute-start = (f32[1024,64]{1,0:T(8,128)S(1)}, f32[1024,64]{1,0:T(8,128)S(1)}, u32[]{:S(2)}, u32[]{:S(2)}) collective-permute-start(f32[1024,64]{1,0:T(8,128)S(1)} %get-tuple-element.7), channel_id=1, source_target_pairs={{0,16},{4,20},{8,24},{12,28},{16,0},{20,4},{24,8},{28,12},{1,17},{... | collective-permute-start | bytes 786440 | tf_op jit(solution)/shard_map/ppermute | solution.py:153
  21.3 29.2 %collective-permute-start.1 = (f32[1024,64]{0,1:T(8,128)S(1)}, f32[1024,64]{0,1:T(8,128)S(1)}, u32[]{:S(2)}, u32[]{:S(2)}) collective-permute-start(f32[1024,64]{0,1:T(8,128)S(1)} %get-tuple-element.3), channel_id=1, source_target_pairs={{0,16},{4,20},{8,24},{12,28},{16,0},{20,4},{24,8},{28,12},{1,17},{... | collective-permute-start | bytes 786440 | tf_op jit(solution)/shard_map/ppermute | solution.py:153
where the time goes:
time: 52.5 us; the launch traced here: 52.3 us
  blocking collectives  21.4 us (41%)
  waiting for transfers between devices  12.2 us (23%)
  Pallas kernels  7.83 us (15%)
  matrix products  6.25 us (12%)
  starting transfers between devices  2.16 us (4%)
  local copies, waits for them, and re-layouts  1.54 us (3%)
  between operations  0.74 us (1%)
    all_gather x2, blocking collectives, one_round(): pieces = lax.all_gather(rotate[None], 'wide', axis=0, tiled=True)  21.4 us
    ppermute x2, waiting for transfers between devices, from_partner(): lax.ppermute(shard, axis, [(i, i ^ 1 << bit) for i in range(lax.axis_size...  12.2 us
    pallas_call x2, Pallas kernels, cayley_sweeps(): pl.pallas_call(functools.partial(solve_kernel, plans), out_shape=jax.Shap...  7.83 us
    dot_general x2, matrix products, one_round(): jnp.einsum('nba,nbc->nac', pieces, row_slab, precision=lax.Precision.HIGH...  2.85 us
    dot_general x2, matrix products, one_round(): basis = jnp.dot(basis, rotate, precision=lax.Precision.HIGHEST)  2.2 us
    ppermute x2, starting transfers between devices, from_partner(): lax.ppermute(shard, axis, [(i, i ^ 1 << bit) for i in range(lax.axis_size...  2.16 us
    dot_general x2, matrix products, one_round(): columns = jnp.dot(current, rotate, precision=lax.Precision.HIGHEST)  1.2 us
  transfers between devices with their start and end apart: 2, of which 1 were waited for; matrix products, arithmetic and copies ran while one was open for 6% of the time, Pallas kernels for 7%

commit v1 on v0

--- a/solution.py
+++ b/solution.py
@@ -135,69 +135,128 @@
 PLANS = ((schedule(4.0, 4),) * SWEEPS, (schedule(0.8, 3),) * SWEEPS)
 
 
-def solve_kernel(plans, block_ref, q_ref, m_ref):
-    solve_into([block_ref[0]], plans, m_ref, q_ref)
-
-
-def cayley_sweeps(pair_block, plans):
-    n = pair_block.shape[0]
+def halves(x):
+    high = x.astype(jnp.bfloat16)
+    return high, (x - high.astype(jnp.float32)).astype(jnp.bfloat16)
+
+
+def quick(a, b):
+    n = b.shape[1]
+    a_high, a_low = halves(a)
+    wide = jnp.concatenate(halves(b), axis=1)
+    both = jnp.dot(a_high, wide, preferred_element_type=jnp.float32) + jnp.dot(
+        a_low, wide, preferred_element_type=jnp.float32
+    )
+    return both[:, :n] + both[:, n:]
+
+
+def pair_up(first, last, cross, n):
+    row = lax.broadcasted_iota(jnp.int32, (n, n), 0) < n // 2
+    col = lax.broadcasted_iota(jnp.int32, (n, n), 1) < n // 2
+    corner = jnp.where(jnp.logical_and(jnp.logical_not(row), col), cross, 0.0)
+    return jnp.where(row == col, jnp.where(row, first, last), corner + corner.T)
+
+
+def first_kernel(own_ref, partner_ref, cross_ref, q_ref, block_ref, m_ref):
+    n = own_ref.shape[0]
+    solve_into([own_ref[...], partner_ref[...]], PLANS[0], m_ref, q_ref)
+    cross = product(q_ref[1].T, product(cross_ref[...], q_ref[0]))
+    block_ref[0] = pair_up(m_ref[0], m_ref[1], cross, n)
+    block_ref[1] = pair_up(m_ref[1], m_ref[0], cross.T, n)
+
+
+def second_kernel(block_ref, q_ref, turn_ref, basis_ref, second_ref, m_ref):
+    n = block_ref.shape[1]
+    half = n // 2
+    solve_into([block_ref[0], block_ref[1]], PLANS[1], m_ref, second_ref)
+    turn_ref[0] = second_ref[0].T
+    turn_ref[1] = second_ref[1].T
+    col = lax.broadcasted_iota(jnp.int32, (n, n), 1) < half
+    mine = second_ref[0]
+    basis_ref[0] = quick(jnp.where(col, q_ref[0], 0.0), mine)
+    basis_ref[1] = quick(jnp.where(col, 0.0, q_ref[1]), mine)
+
+
+def rows_of(pair, n):
+    return pl.ds(pl.multiple_of(pair * n, n), n)
+
+
+def columns_kernel(masks, far, factor_ref, moved_ref, basis_ref, *refs):
+    turn_refs, (mixed_ref, out_ref) = refs[:-2], refs[-2:]
+    n = factor_ref.shape[1]
+    half = n // 2
+    me = lax.axis_index("wide")
+    out_ref[...] = jnp.zeros_like(out_ref)
+    out_ref[rows_of(me, n), :] = basis_ref[0]
+    out_ref[rows_of(me ^ far, n), :] = basis_ref[1]
+    first, last = basis_ref[0], basis_ref[1]
+    for mask, turn_ref in zip(masks, turn_refs):
+        turned = []
+        for side in range(2):
+            pair = me ^ mask ^ (far * side)
+            rows = rows_of(pair, n)
+            columns = quick(factor_ref[rows, :], first) + quick(moved_ref[rows, :], last)
+            turned.append(quick(turn_ref[side].T, columns))
+        for side in range(2):
+            pair = me ^ mask ^ (far * side)
+            mixed_ref[rows_of(pair, n), :] = jnp.concatenate(
+                [turned[side][:half], turned[1 - side][half:]], axis=0
+            )
+
+
+def rows_kernel(masks, far, mixed_ref, *refs):
+    turn_refs, out_ref = refs[:-1], refs[-1]
+    n = mixed_ref.shape[1]
+    me = lax.axis_index("wide")
+    for mask, turn_ref in zip(masks, turn_refs):
+        for side in range(2):
+            rows = rows_of(me ^ mask ^ (far * side), n)
+            out_ref[rows, :] = quick(turn_ref[side], mixed_ref[rows, :])
+
+
+def call(kernel, out_shape, scratch_shapes, flops, *args):
     return pl.pallas_call(
-        functools.partial(solve_kernel, plans),
-        out_shape=jax.ShapeDtypeStruct((1, n, n), jnp.float32),
-        scratch_shapes=[pltpu.VMEM((1, n, n), jnp.float32)],
-        compiler_params=pltpu.CompilerParams(vmem_limit_bytes=32 * 1024 * 1024),
-    )(pair_block[None])[0]
-
-
-def from_partner(shard, axis, bit):
-    return lax.ppermute(shard, axis, [(i, i ^ 1 << bit) for i in range(lax.axis_size(axis))])
-
-
-def trade_rows(current, wide_count, width_half):
-    order_size, pair_span = current.shape
-    split_view = current.reshape(2, wide_count // 2, 2, width_half, pair_span)
-    joined = jnp.concatenate([split_view[:, :, :1], split_view[::-1, :, 1:]], axis=2)
-    return joined.reshape(order_size, pair_span)
-
-
-def one_round(current, basis, my_pair, plans):
-    order_size, pair_span = current.shape
-    pair_block = lax.dynamic_slice_in_dim(current, my_pair * pair_span, pair_span, 0)
-    rotate = cayley_sweeps(pair_block, plans)
-    columns = jnp.dot(current, rotate, precision=lax.Precision.HIGHEST)
-    pieces = lax.all_gather(rotate[None], "wide", axis=0, tiled=True)
-    how_many = pieces.shape[0]
-    row_slab = columns
-    row_slab = row_slab.reshape(how_many, pair_span, pair_span)
-    updated = jnp.einsum("nba,nbc->nac", pieces, row_slab, precision=lax.Precision.HIGHEST)
-    current = lax.dynamic_update_slice_in_dim(
-        columns, updated.reshape(how_many * pair_span, pair_span), jnp.int32(0) * pair_span, 0
-    )
-    basis = jnp.dot(basis, rotate, precision=lax.Precision.HIGHEST)
-    return (current, basis)
+        kernel,
+        out_shape=out_shape,
+        scratch_shapes=scratch_shapes,
+        compiler_params=pltpu.CompilerParams(vmem_limit_bytes=48 * 1024 * 1024),
+        cost_estimate=pl.CostEstimate(flops=flops, bytes_accessed=2**20, transcendentals=0),
+    )(*args)
+
+
+def swap(shard, mask):
+    return lax.ppermute(shard, "wide", [(i, i ^ mask) for i in range(lax.axis_size("wide"))])
 
 
 def body(factor):
     wide_count = lax.axis_size("wide")
-    my_pair = lax.axis_index("wide")
-    order_size, pair_span = factor.shape
-    width_half = pair_span // 2
-    row_index = lax.broadcasted_iota(jnp.int32, (order_size, pair_span), 0)
-    col_index = lax.broadcasted_iota(jnp.int32, (order_size, pair_span), 1) + my_pair * pair_span
-    basis = (row_index == col_index).astype(jnp.float32)
-    current = factor
-    for repeat in range(2):
-        if repeat == 1:
-            moved_factor, moved_basis = from_partner(
-                (current[:, width_half:], basis[:, width_half:]),
-                "wide",
-                wide_count.bit_length() - 2,
-            )
-            current = jnp.concatenate([current[:, :width_half], moved_factor], axis=1)
-            basis = jnp.concatenate([basis[:, :width_half], moved_basis], axis=1)
-            current = trade_rows(current, wide_count, width_half)
-        current, basis = one_round(current, basis, my_pair, PLANS[repeat])
-    return (current, basis)
+    far = wide_count // 2
+    me = lax.axis_index("wide")
+    order_size, n = factor.shape
+    two = jax.ShapeDtypeStruct((2, n, n), jnp.float32)
+    tall = jax.ShapeDtypeStruct((order_size, n), jnp.float32)
+    scratch = pltpu.VMEM((2, n, n), jnp.float32)
+    own = lax.dynamic_slice_in_dim(factor, me * n, n, 0)
+    cross = lax.dynamic_slice_in_dim(factor, (me ^ far) * n, n, 0)
+    partner = swap(own, far)
+    moved = swap(lax.optimization_barrier((factor, partner))[0], far)
+    turns, blocks = call(first_kernel, (two, two), [scratch], 2**33, own, partner, cross)
+
+    def spread(pieces):
+        bit = far // 2
+        while bit:
+            pieces = pieces + [(mask | bit, swap(piece, bit)) for mask, piece in pieces]
+            bit //= 2
+        return [mask for mask, _ in pieces], [piece for _, piece in pieces]
+
+    masks, all_first = spread([(0, turns)])
+    second, basis = call(second_kernel, (two, two), [scratch, scratch], 2**33, blocks, turns)
+    masks, all_second = spread([(0, second)])
+    mixed, eigen_basis = call(
+        functools.partial(columns_kernel, masks, far), (tall, tall), [], 2**31, factor, moved, basis, *all_first
+    )
+    rotated = call(functools.partial(rows_kernel, masks, far), tall, [], 2**30, mixed, *all_second)
+    return (rotated, eigen_basis)
 
 
 def solution(mesh):

time: 52.5 us -> 33.2 us (0.63)
  blocking collectives: 21.4 us -> 0 us
  Pallas kernels: 7.83 us -> 17.5 us
  matrix products: 6.25 us -> 0 us
  waiting for transfers between devices: 12.2 us -> 6.17 us
  starting transfers between devices: 2.16 us -> 7.72 us
  local copies, waits for them, and re-layouts: 1.54 us -> 0.89 us
    all_gather x2 -> x0, blocking collectives: 21.4 us -> none  [one_round(): pieces = lax.all_gather(rotate[None], 'wide', axis=0, tiled=True)]
    pallas_call x2 -> x4, Pallas kernels: 7.83 us -> 17.5 us  [call(): pl.pallas_call(kernel, out_shape=out_shape, scratch_shapes=scratch_shapes...]
    dot_general x6 -> x0, matrix products: 6.25 us -> none  [the longest x2 2.85 us: one_round(): jnp.einsum('nba,nbc->nac', pieces, row_slab, precision=lax.Precision.HIGH...]
    ppermute x2 -> x8, waiting for transfers between devices: 12.2 us -> 6.17 us  [swap(): lax.ppermute(shard, 'wide', [(i, i ^ mask) for i in range(lax.axis_size('...]
    ppermute x2 -> x8, starting transfers between devices: 2.16 us -> 7.72 us  [swap(): lax.ppermute(shard, 'wide', [(i, i ^ mask) for i in range(lax.axis_size('...]
    unnamed x2, local copies, waits for them, and re-layouts: 1.03 us -> 0.01 us
    dynamic_slice x0 -> x1, local copies, waits for them, and re-layouts: none -> 0.89 us  [body(): cross = lax.dynamic_slice_in_dim(factor, (me ^ far) * n, n, 0)]
  transfers between devices with their start and end apart: 2 -> 8, of which waited for: 1 -> 2; matrix products, arithmetic and copies ran while one was open for 6% -> 0% of each run, Pallas kernels for 7% -> 26%
where the time goes in v1:
time: 33.2 us; the launch traced here: 33 us
  Pallas kernels  17.5 us (53%)
  starting transfers between devices  7.72 us (23%)
  waiting for transfers between devices  6.17 us (19%)
  local copies, waits for them, and re-layouts  0.89 us (3%)
  between operations  0.67 us (2%)
    pallas_call x4, Pallas kernels, call(): pl.pallas_call(kernel, out_shape=out_shape, scratch_shapes=scratch_shapes...  17.5 us
    ppermute x8, starting transfers between devices, swap(): lax.ppermute(shard, 'wide', [(i, i ^ mask) for i in range(lax.axis_size('...  7.72 us
    ppermute x8, waiting for transfers between devices, swap(): lax.ppermute(shard, 'wide', [(i, i ^ mask) for i in range(lax.axis_size('...  6.17 us
    dynamic_slice x1, local copies, waits for them, and re-layouts, body(): cross = lax.dynamic_slice_in_dim(factor, (me ^ far) * n, n, 0)  0.89 us
  transfers between devices with their start and end apart: 8, of which 2 were waited for; matrix products, arithmetic and copies ran while one was open for 0% of the time, Pallas kernels for 26%

profile of v1, /device:TPU:0, one launch (start us, length us, event | category | flops | bytes accessed | tf_op | source)
XLA Modules:
  0.0 33.0 jit_solution(13756379099358028059)
XLA Ops:
  0.6 0.9 %constant_dynamic-slice_fusion = (f32[128,128]{1,0:T(8,128)S(1)}, f32[128,128]{1,0:T(8,128)S(1)}) fusion(f32[1024,128]{1,0:T(8,128)} %factor_ref.1, s32[]{:T(128)S(6)} %select_n.7, s32[]{:T(128)S(6)} %select_n.6), kind=kLoop, calls=%fused_computation | loop fusion | bytes 262152 | tf_op jit(solution)/shard_map/dynamic_slice | solution.py:240
  1.5 3.0 %collective-permute-start = (f32[128,128]{1,0:T(8,128)S(1)}, f32[128,128]{1,0:T(8,128)S(1)}, u32[]{:S(2)}, u32[]{:S(2)}) collective-permute-start(f32[128,128]{1,0:T(8,128)S(1)} %get-tuple-element.17.own_ref), channel_id=1, source_target_pairs={{0,16},{4,20},{8,24},{12,28},{16,0},{20,4},{24,8},{28,12},{1,17},{... | collective-permute-start | bytes 196616 | tf_op jit(solution)/shard_map/ppermute | solution.py:228
  4.6 2.2 %collective-permute-done.partner_ref = f32[128,128]{1,0:T(8,128)S(1)} collective-permute-done((f32[128,128]{1,0:T(8,128)S(1)}, f32[128,128]{1,0:T(8,128)S(1)}, u32[]{:S(2)}, u32[]{:S(2)}) %collective-permute-start) | collective-permute-done | bytes 65568 | tf_op jit(solution)/shard_map/ppermute | solution.py:228
  6.8 0.0 copy-start
  6.8 7.6 %shard_map.30 = (f32[2,128,128]{2,1,0:T(8,128)S(1)}, f32[2,128,128]{2,1,0:T(8,128)S(1)}) custom-call(f32[128,128]{1,0:T(8,128)S(1)} %get-tuple-element.17.own_ref, f32[128,128]{1,0:T(8,128)S(1)} %collective-permute-done.partner_ref, f32[128,128]{1,0:T(8,128)S(1)} %get-tuple-element.16.cross_ref), custom_call_target="tpu_custom_call" | custom-call | flops 8589934592 | bytes 1048576 | tf_op jit(solution)/shard_map/pallas_call | solution.py:218
  14.4 2.1 %collective-permute-start.2 = (f32[2,128,128]{2,1,0:T(8,128)S(1)}, f32[2,128,128]{2,1,0:T(8,128)S(1)}, u32[]{:S(2)}, u32[]{:S(2)}) collective-permute-start(f32[2,128,128]{2,1,0:T(8,128)S(1)} %get-tuple-element.11.q_ref.refs_0_), channel_id=1, source_target_pairs={{0,8},{4,12},{8,0},{12,4},{16,24},{20,28},{24,16},{28,20},{1,9},{5... | collective-permute-start | bytes 393224 | tf_op jit(solution)/shard_map/ppermute | solution.py:228
  16.5 0.0 copy-done
  16.5 1.5 %collective-permute-start.1 = (f32[1024,128]{1,0:T(8,128)S(1)}, f32[1024,128]{1,0:T(8,128)S(1)}, u32[]{:S(2)}, u32[]{:S(2)}) collective-permute-start(f32[1024,128]{1,0:T(8,128)S(1)} %copy-done), channel_id=1, source_target_pairs={{0,16},{4,20},{8,24},{12,28},{16,0},{20,4},{24,8},{28,12},{1,17},{... | collective-permute-start | bytes 1572872 | tf_op jit(solution)/shard_map/ppermute | solution.py:228
  18.0 5.9 %shard_map.31 = (f32[2,128,128]{2,1,0:T(8,128)S(1)}, f32[2,128,128]{2,1,0:T(8,128)S(1)}) custom-call(f32[2,128,128]{2,1,0:T(8,128)S(1)} %get-tuple-element.10.block_ref, f32[2,128,128]{2,1,0:T(8,128)S(1)} %get-tuple-element.11.q_ref.refs_0_), custom_call_target="tpu_custom_call" | custom-call | flops 8589934592 | bytes 1048576 | tf_op jit(solution)/shard_map/pallas_call | solution.py:218
  23.9 0.6 %collective-permute-start.5 = (f32[2,128,128]{2,1,0:T(8,128)S(1)}, f32[2,128,128]{2,1,0:T(8,128)S(1)}, u32[]{:S(2)}, u32[]{:S(2)}) collective-permute-start(f32[2,128,128]{2,1,0:T(8,128)S(1)} %get-tuple-element.14.refs_0_), channel_id=1, source_target_pairs={{0,8},{4,12},{8,0},{12,4},{16,24},{20,28},{24,16},{28,20},{1,9},{5... | collective-permute-start | bytes 393224 | tf_op jit(solution)/shard_map/ppermute | solution.py:228
  24.5 0.0 collective-permute-start.3
  24.5 0.0 collective-permute-done.2.refs_1_
  24.5 0.5 %collective-permute-start.4 = (f32[2,128,128]{2,1,0:T(8,128)S(1)}, f32[2,128,128]{2,1,0:T(8,128)S(1)}, u32[]{:S(2)}, u32[]{:S(2)}) collective-permute-start(f32[2,128,128]{2,1,0:T(8,128)S(1)} %collective-permute-done.2.refs_1_), channel_id=1, source_target_pairs={{0,4},{4,0},{8,12},{12,8},{16,20},{20,16},{24,28},{28,24},{1,5},{5... | collective-permute-start | bytes 393224 | tf_op jit(solution)/shard_map/ppermute | solution.py:228
  25.1 0.0 collective-permute-start.6
  25.1 3.9 %collective-permute-done.5.refs_1_ = f32[2,128,128]{2,1,0:T(8,128)S(1)} collective-permute-done((f32[2,128,128]{2,1,0:T(8,128)S(1)}, f32[2,128,128]{2,1,0:T(8,128)S(1)}, u32[]{:S(2)}, u32[]{:S(2)}) %collective-permute-start.5) | collective-permute-done | bytes 131104 | tf_op jit(solution)/shard_map/ppermute | solution.py:228
  29.0 0.0 collective-permute-start.7
  29.0 0.0 collective-permute-done.3.refs_2_
  29.0 0.0 collective-permute-done.4.refs_3_
  29.0 0.0 collective-permute-done.1.moved_ref
  29.0 2.8 %shard_map.32 = (f32[1024,128]{1,0:T(8,128)S(1)}, f32[1024,128]{1,0:T(8,128)}) custom-call(f32[1024,128]{1,0:T(8,128)S(1)} %copy-done, f32[1024,128]{1,0:T(8,128)S(1)} %collective-permute-done.1.moved_ref, f32[2,128,128]{2,1,0:T(8,128)S(1)} %get-tuple-element.12.basis_ref, f32[2,128,128]{2,1,0:T(8,128)S(1)} %get-tuple-element.11.q_ref.refs_0_, ...), custom_call_target="tpu_custom_call" | custom-call | flops 2147483648 | bytes 1048576 | tf_op jit(solution)/shard_map/pallas_call | solution.py:218
  31.8 0.0 collective-permute-done.6.refs_2_
  31.8 0.0 collective-permute-done.7.refs_3_
  31.8 1.2 %shard_map.33 = f32[1024,128]{1,0:T(8,128)} custom-call(f32[1024,128]{1,0:T(8,128)S(1)} %get-tuple-element.13.mixed_ref, f32[2,128,128]{2,1,0:T(8,128)S(1)} %get-tuple-element.14.refs_0_, f32[2,128,128]{2,1,0:T(8,128)S(1)} %collective-permute-done.5.refs_1_, f32[2,128,128]{2,1,0:T(8,128)S(1)} %collective-permute-done.6.refs_2_, ...), custom_call_target="tpu_custom_call" | custom-call | flops 1073741824 | bytes 1048576 | tf_op jit(solution)/shard_map/pallas_call | solution.py:218
Async XLA Ops:
  1.5 5.3 %collective-permute-start = (f32[128,128]{1,0:T(8,128)S(1)}, f32[128,128]{1,0:T(8,128)S(1)}, u32[]{:S(2)}, u32[]{:S(2)}) collective-permute-start(f32[128,128]{1,0:T(8,128)S(1)} %get-tuple-element.17.own_ref), channel_id=1, source_target_pairs={{0,16},{4,20},{8,24},{12,28},{16,0},{20,4},{24,8},{28,12},{1,17},{... | collective-permute-start | bytes 196616 | tf_op jit(solution)/shard_map/ppermute | solution.py:228
  6.8 9.7 %copy-start = (f32[1024,128]{1,0:T(8,128)S(1)}, f32[1024,128]{1,0:T(8,128)}, u32[]{:S(2)}) copy-start(f32[1024,128]{1,0:T(8,128)} %factor_ref.1) | copy-start | bytes 1572868
  14.4 10.1 %collective-permute-start.2 = (f32[2,128,128]{2,1,0:T(8,128)S(1)}, f32[2,128,128]{2,1,0:T(8,128)S(1)}, u32[]{:S(2)}, u32[]{:S(2)}) collective-permute-start(f32[2,128,128]{2,1,0:T(8,128)S(1)} %get-tuple-element.11.q_ref.refs_0_), channel_id=1, source_target_pairs={{0,8},{4,12},{8,0},{12,4},{16,24},{20,28},{24,16},{28,20},{1,9},{5... | collective-permute-start | bytes 393224 | tf_op jit(solution)/shard_map/ppermute | solution.py:228
  16.5 12.5 %collective-permute-start.1 = (f32[1024,128]{1,0:T(8,128)S(1)}, f32[1024,128]{1,0:T(8,128)S(1)}, u32[]{:S(2)}, u32[]{:S(2)}) collective-permute-start(f32[1024,128]{1,0:T(8,128)S(1)} %copy-done), channel_id=1, source_target_pairs={{0,16},{4,20},{8,24},{12,28},{16,0},{20,4},{24,8},{28,12},{1,17},{... | collective-permute-start | bytes 1572872 | tf_op jit(solution)/shard_map/ppermute | solution.py:228
  23.9 5.0 %collective-permute-start.5 = (f32[2,128,128]{2,1,0:T(8,128)S(1)}, f32[2,128,128]{2,1,0:T(8,128)S(1)}, u32[]{:S(2)}, u32[]{:S(2)}) collective-permute-start(f32[2,128,128]{2,1,0:T(8,128)S(1)} %get-tuple-element.14.refs_0_), channel_id=1, source_target_pairs={{0,8},{4,12},{8,0},{12,4},{16,24},{20,28},{24,16},{28,20},{1,9},{5... | collective-permute-start | bytes 393224 | tf_op jit(solution)/shard_map/ppermute | solution.py:228
  24.5 4.4 %collective-permute-start.3 = (f32[2,128,128]{2,1,0:T(8,128)S(1)}, f32[2,128,128]{2,1,0:T(8,128)S(1)}, u32[]{:S(2)}, u32[]{:S(2)}) collective-permute-start(f32[2,128,128]{2,1,0:T(8,128)S(1)} %get-tuple-element.11.q_ref.refs_0_), channel_id=1, source_target_pairs={{0,4},{4,0},{8,12},{12,8},{16,20},{20,16},{24,28},{28,24},{1,5},{5... | collective-permute-start | bytes 393224 | tf_op jit(solution)/shard_map/ppermute | solution.py:228
  24.5 4.4 %collective-permute-start.4 = (f32[2,128,128]{2,1,0:T(8,128)S(1)}, f32[2,128,128]{2,1,0:T(8,128)S(1)}, u32[]{:S(2)}, u32[]{:S(2)}) collective-permute-start(f32[2,128,128]{2,1,0:T(8,128)S(1)} %collective-permute-done.2.refs_1_), channel_id=1, source_target_pairs={{0,4},{4,0},{8,12},{12,8},{16,20},{20,16},{24,28},{28,24},{1,5},{5... | collective-permute-start | bytes 393224 | tf_op jit(solution)/shard_map/ppermute | solution.py:228
  25.1 6.7 %collective-permute-start.6 = (f32[2,128,128]{2,1,0:T(8,128)S(1)}, f32[2,128,128]{2,1,0:T(8,128)S(1)}, u32[]{:S(2)}, u32[]{:S(2)}) collective-permute-start(f32[2,128,128]{2,1,0:T(8,128)S(1)} %get-tuple-element.14.refs_0_), channel_id=1, source_target_pairs={{0,4},{4,0},{8,12},{12,8},{16,20},{20,16},{24,28},{28,24},{1,5},{5... | collective-permute-start | bytes 393224 | tf_op jit(solution)/shard_map/ppermute | solution.py:228
  29.0 2.8 %collective-permute-start.7 = (f32[2,128,128]{2,1,0:T(8,128)S(1)}, f32[2,128,128]{2,1,0:T(8,128)S(1)}, u32[]{:S(2)}, u32[]{:S(2)}) collective-permute-start(f32[2,128,128]{2,1,0:T(8,128)S(1)} %collective-permute-done.5.refs_1_), channel_id=1, source_target_pairs={{0,4},{4,0},{8,12},{12,8},{16,20},{20,16},{24,28},{28,24},{1,5},{5... | collective-permute-start | bytes 393224 | tf_op jit(solution)/shard_map/ppermute | solution.py:228

commit v2 on v1

v2 whole, which is shorter than its diff:
```python
import functools
import jax
import jax.numpy as jnp
from jax import lax
from jax.experimental import pallas as pl
from jax.experimental.pallas import tpu as pltpu
from jax.sharding import PartitionSpec as P

SWEEPS = 3
FLOOR = 0.01
TOLERANCE = 2e-6


def schedule(bound, steps=None, goal=1e-6):
    theta = bound / (2.0 + bound)
    mus = []
    while len(mus) < steps if steps else theta > goal:
        mus.append(2.0 / (2.0 - theta * theta))
        theta = theta * theta / (2.0 - theta * theta)
    return 1.0 / (1.0 + 0.5 * bound), tuple(mus)


def split(x):
    high = x.astype(jnp.bfloat16)
    x = x - high.astype(jnp.float32)
    middle = x.astype(jnp.bfloat16)
    return high, middle, (x - middle.astype(jnp.float32)).astype(jnp.bfloat16)


def product(a, b):
    n = b.shape[1]
    a_high, a_middle, a_low = split(a)
    b_high, b_middle, b_low = split(b)
    wide = jnp.concatenate([b_high, b_middle], axis=1)
    most = jnp.dot(
        jnp.concatenate([a_high, a_middle], axis=1),
        jnp.concatenate([wide, wide], axis=0),
        preferred_element_type=jnp.float32,
    )
    rest = jnp.dot(
        jnp.concatenate([a_high, a_low], axis=1),
        jnp.concatenate([b_low, b_high], axis=0),
        preferred_element_type=jnp.float32,
    )
    return most[:, :n] + (most[:, n:] + rest)


def exact(a, b):
    return jnp.dot(a, b, precision=lax.Precision.HIGHEST, preferred_element_type=jnp.float32)


def identity_of(n):
    row = lax.broadcasted_iota(jnp.int32, (n, n), 0)
    col = lax.broadcasted_iota(jnp.int32, (n, n), 1)
    return (row == col).astype(jnp.float32)


def half_skew(m, eye):
    kept = m * eye
    spread = jnp.sum(kept, axis=0, keepdims=True) - jnp.sum(kept, axis=1, keepdims=True)
    ratios = m * spread / (spread * spread + 2.0 * m * m + FLOOR)
    return 0.25 * (ratios - ratios.T)


def sure_sweep(m, qt, eye):
    n = m.shape[0]
    a = half_skew(m, eye)
    system = eye - exact(a, a)
    scale, mus = schedule(n * n / 32.0)

    def newton(_, y):
        return y + exact(y, eye - exact(system, y))

    y = lax.fori_loop(0, len(mus) + 6, newton, scale * eye)
    x = exact(y, eye + a)
    x = x + exact(x, eye - (x - exact(a, x)))
    turn = 2.0 * x - eye
    return exact(turn.T, exact(m, turn)), exact(turn.T, qt)


def solve(blocks, plans, eye, keep):
    n = eye.shape[0]
    some = range(len(blocks))
    ms, qts = list(blocks), None
    worst = jnp.zeros((1, n), jnp.float32)
    for index, (scale, mus) in enumerate(plans):
        carried = keep or index + 1 < len(plans)
        skews = [half_skew(m, eye) for m in ms]
        if carried:
            firsts = [product(jnp.concatenate([a, m], axis=0), a) for a, m in zip(skews, ms)]
        else:
            firsts = [product(a, a) for a in skews]
        errors = [(1.0 - scale) * eye + scale * first[:n] for first in firsts]
        stacks = [scale * (eye - a) for a in skews]
        if carried:
            stacks = [
                jnp.concatenate([stack, scale * (m + first[n:])], axis=0)
                for stack, m, first in zip(stacks, ms, firsts)
            ]
        for mu in mus:
            steps = [
                product(jnp.concatenate([error, stack], axis=0), error)
                for error, stack in zip(errors, stacks)
            ]
            errors = [(1.0 - mu) * eye + mu * step[:n] for step in steps]
            stacks = [mu * (stack + step[n:]) for stack, step in zip(stacks, steps)]
        for error in errors:
            worst = worst + jnp.sum(error * error, axis=0, keepdims=True)
        backs = [2.0 * stack[:n] - eye for stack in stacks]
        rights = [[] for _ in some]
        if carried:
            rights = [[2.0 * stack[n:] - m] for stack, m in zip(stacks, ms)]
        if qts is not None:
            rights = [right + [qt] for right, qt in zip(rights, qts)]
        turned = [
            product(back, jnp.concatenate(right, axis=1)) for back, right in zip(backs, rights)
        ]
        qts = backs if qts is None else [both[:, -n:] for both in turned]
        if carried:
            ms = [both[:, :n] for both in turned]
    return ms, qts, worst


def settled(worst):
    return jnp.sum(worst) <= TOLERANCE * TOLERANCE * worst.shape[1]


def solve_surely(blocks, m_ref, qt_ref, eye):
    for k in range(len(blocks)):
        m_ref[k] = blocks[k]
        qt_ref[k] = eye

    def again(step, carry):
        k = step // SWEEPS
        m_ref[k], qt_ref[k] = sure_sweep(m_ref[k], qt_ref[k], eye)
        return carry

    lax.fori_loop(0, SWEEPS * len(blocks), again, 0)


PLANS = ((schedule(4.0, 4),) * SWEEPS, (schedule(0.8, 3),) * SWEEPS)


def halves(x):
    high = x.astype(jnp.bfloat16)
    return high, (x - high.astype(jnp.float32)).astype(jnp.bfloat16)


def quick(a, b):
    n = b.shape[1]
    wide = jnp.concatenate(halves(b), axis=1)
    both = jnp.dot(
        jnp.concatenate(halves(a), axis=1),
        jnp.concatenate([wide, wide], axis=0),
        preferred_element_type=jnp.float32,
    )
    return both[:, :n] + both[:, n:]


def pair_up(first, last, cross):
    n = first.shape[0]
    row = lax.broadcasted_iota(jnp.int32, (n, n), 0) < n // 2
    col = lax.broadcasted_iota(jnp.int32, (n, n), 1) < n // 2
    corner = jnp.where(jnp.logical_and(jnp.logical_not(row), col), cross, 0.0)
    return jnp.where(row == col, jnp.where(row, first, last), corner + corner.T)


def rows_of(pair, n):
    return pl.ds(pl.multiple_of(pair * n, n), n)


def first_kernel(own_ref, partner_ref, cross_ref, qt_ref, block_ref, m_ref):
    n = own_ref.shape[0]
    eye = identity_of(n)
    cross = cross_ref[...]

    def finish(ms, qts):
        moved = product(qts[1], product(cross, qts[0].T))
        block_ref[0] = pair_up(ms[0], ms[1], moved)
        block_ref[1] = pair_up(ms[1], ms[0], moved.T)

    blocks = [own_ref[...], partner_ref[...]]
    ms, qts, worst = solve(blocks, PLANS[0], eye, True)
    qt_ref[0], qt_ref[1] = qts
    finish(ms, qts)

    @pl.when(jnp.logical_not(settled(worst)))
    def _():
        solve_surely([own_ref[...], partner_ref[...]], m_ref, qt_ref, eye)
        finish([m_ref[0], m_ref[1]], [qt_ref[0], qt_ref[1]])


def second_kernel(block_ref, qt_ref, m_ref):
    eye = identity_of(block_ref.shape[1])
    _, (qt_ref[0], qt_ref[1]), worst = solve([block_ref[0], block_ref[1]], PLANS[1], eye, False)

    @pl.when(jnp.logical_not(settled(worst)))
    def _():
        solve_surely([block_ref[0], block_ref[1]], m_ref, qt_ref, eye)


def columns_kernel(masks, far, factor_ref, moved_ref, second_ref, *refs):
    turn_refs, (mixed_ref, out_ref) = refs[:-2], refs[-2:]
    n = factor_ref.shape[1]
    half = n // 2
    me = lax.axis_index("wide")
    pairs = [[me ^ mask ^ (far * side) for side in range(2)] for mask in masks]
    row = lax.broadcasted_iota(jnp.int32, (n, n), 0) < half
    turn = second_ref[0].T
    first = quick(jnp.where(row, turn_refs[0][0], 0.0).T, turn)
    last = quick(jnp.where(row, 0.0, turn_refs[0][1]).T, turn)
    out_ref[...] = jnp.zeros_like(out_ref)
    out_ref[rows_of(pairs[0][0], n), :] = first
    out_ref[rows_of(pairs[0][1], n), :] = last
    both = jnp.concatenate([first, last], axis=0)
    for couple in pairs:
        for pair in couple:
            rows = rows_of(pair, n)
            columns = jnp.concatenate([factor_ref[rows, :], moved_ref[rows, :]], axis=1)
            mixed_ref[rows, :] = quick(columns, both)
    for couple, turn_ref in zip(pairs, turn_refs):
        near, away = [
            quick(turn_ref[side], mixed_ref[rows_of(pair, n), :]) for side, pair in enumerate(couple)
        ]
        mixed_ref[rows_of(couple[0], n), :] = jnp.concatenate([near[:half], away[half:]], axis=0)
        mixed_ref[rows_of(couple[1], n), :] = jnp.concatenate([away[:half], near[half:]], axis=0)


def rows_kernel(masks, far, mixed_ref, *refs):
    turn_refs, out_ref = refs[:-1], refs[-1]
    n = mixed_ref.shape[1]
    me = lax.axis_index("wide")
    for mask, turn_ref in zip(masks, turn_refs):
        for side in range(2):
            rows = rows_of(me ^ mask ^ (far * side), n)
            out_ref[rows, :] = quick(turn_ref[side], mixed_ref[rows, :])


def call(kernel, out_shape, scratch_shapes, flops, *args):
    return pl.pallas_call(
        kernel,
        out_shape=out_shape,
        scratch_shapes=scratch_shapes,
        compiler_params=pltpu.CompilerParams(vmem_limit_bytes=48 * 1024 * 1024),
        cost_estimate=pl.CostEstimate(flops=flops, bytes_accessed=2**20, transcendentals=0),
    )(*args)


def swap(shard, mask):
    return lax.ppermute(shard, "wide", [(i, i ^ mask) for i in range(lax.axis_size("wide"))])


def spread(piece, far, gate=None):
    pieces = [(0, piece)]
    bit = far // 2
    while bit:
        fresh = []
        for mask, held in pieces:
            if gate is not None and mask and bit == 1:
                held = lax.optimization_barrier((held, gate))[0]
            fresh.append((mask | bit, swap(held, bit)))
        pieces = pieces + fresh
        bit //= 2
    return [mask for mask, _ in pieces], [held for _, held in pieces]


def body(factor):
    far = lax.axis_size("wide") // 2
    me = lax.axis_index("wide")
    order_size, n = factor.shape
    two = jax.ShapeDtypeStruct((2, n, n), jnp.float32)
    tall = jax.ShapeDtypeStruct((order_size, n), jnp.float32)
    scratch = [pltpu.VMEM((2, n, n), jnp.float32)]
    own = lax.dynamic_slice_in_dim(factor, me * n, n, 0)
    cross = lax.dynamic_slice_in_dim(factor, (me ^ far) * n, n, 0)
    partner = swap(own, far)
    moved = swap(factor, far)
    turns, blocks = call(
        first_kernel, (two, two), scratch, 2**32, own, partner, cross
    )

    second = call(second_kernel, two, scratch, 2**32, blocks)
    masks, all_first = spread(turns, far, second)
    mixed, eigen_basis = call(
        functools.partial(columns_kernel, masks, far),
        (tall, tall),
        [],
        2**20,
        factor,
        moved,
        second,
        *all_first,
    )
    masks, all_second = spread(second, far, mixed)
    rotated = call(functools.partial(rows_kernel, masks, far), tall, [], 2**20, mixed, *all_second)
    return (rotated, eigen_basis)


def solution(mesh):
    return jax.shard_map(
        body,
        mesh=mesh,
        in_specs=(P("layer", "wide"),),
        out_specs=(P("layer", "wide"), P("layer", "wide")),
        check_vma=False,
    )
```

time: 33.2 us -> 26.7 us (0.80)
  Pallas kernels: 17.5 us -> 12 us
  starting transfers between devices: 7.72 us -> 6.78 us
    pallas_call x4, Pallas kernels: 17.5 us -> 12 us  [call(): pl.pallas_call(kernel, out_shape=out_shape, scratch_shapes=scratch_shapes...]
    ppermute x8, starting transfers between devices: 7.72 us -> 6.78 us  [swap(): lax.ppermute(shard, 'wide', [(i, i ^ mask) for i in range(lax.axis_size('...]
  transfers between devices with their start and end apart: 8 -> 8, of which waited for: 2 -> 4; matrix products, arithmetic and copies ran while one was open for 0% -> 0% of each run, Pallas kernels for 26% -> 41%
where the time goes in v2:
time: 26.7 us; the launch traced here: 26.5 us
  Pallas kernels  12 us (45%)
  starting transfers between devices  6.78 us (25%)
  waiting for transfers between devices  6.15 us (23%)
  local copies, waits for them, and re-layouts  0.89 us (3%)
  between operations  0.67 us (3%)
    pallas_call x4, Pallas kernels, call(): pl.pallas_call(kernel, out_shape=out_shape, scratch_shapes=scratch_shapes...  12 us
    ppermute x8, starting transfers between devices, swap(): lax.ppermute(shard, 'wide', [(i, i ^ mask) for i in range(lax.axis_size('...  6.78 us
    ppermute x8, waiting for transfers between devices, swap(): lax.ppermute(shard, 'wide', [(i, i ^ mask) for i in range(lax.axis_size('...  6.15 us
    dynamic_slice x1, local copies, waits for them, and re-layouts, body(): cross = lax.dynamic_slice_in_dim(factor, (me ^ far) * n, n, 0)  0.89 us
  transfers between devices with their start and end apart: 8, of which 4 were waited for; matrix products, arithmetic and copies ran while one was open for 0% of the time, Pallas kernels for 41%

profile of v2, /device:TPU:0, one launch (start us, length us, event | category | flops | bytes accessed | tf_op | source)
XLA Modules:
  0.0 26.5 jit_solution(2907729021854228994)
XLA Ops:
  0.6 0.9 %constant_dynamic-slice_fusion = (f32[128,128]{1,0:T(8,128)S(1)}, f32[128,128]{1,0:T(8,128)S(1)}) fusion(f32[1024,128]{1,0:T(8,128)} %factor_ref.1, s32[]{:T(128)S(6)} %select_n.7, s32[]{:T(128)S(6)} %select_n.6), kind=kLoop, calls=%fused_computation | loop fusion | bytes 262152 | tf_op jit(solution)/shard_map/dynamic_slice | solution.py:275
  1.5 3.0 %collective-permute-start.1 = (f32[128,128]{1,0:T(8,128)S(1)}, f32[128,128]{1,0:T(8,128)S(1)}, u32[]{:S(2)}, u32[]{:S(2)}) collective-permute-start(f32[128,128]{1,0:T(8,128)S(1)} %get-tuple-element.15.own_ref), channel_id=1, source_target_pairs={{0,16},{4,20},{8,24},{12,28},{16,0},{20,4},{24,8},{28,12},{1,17},{... | collective-permute-start | bytes 196616 | tf_op jit(solution)/shard_map/ppermute | solution.py:250
  4.6 0.1 collective-permute-start
  4.6 2.4 %collective-permute-done.1.partner_ref = f32[128,128]{1,0:T(8,128)S(1)} collective-permute-done((f32[128,128]{1,0:T(8,128)S(1)}, f32[128,128]{1,0:T(8,128)S(1)}, u32[]{:S(2)}, u32[]{:S(2)}) %collective-permute-start.1) | collective-permute-done | bytes 65568 | tf_op jit(solution)/shard_map/ppermute | solution.py:250
  7.1 5.0 %shard_map.30 = (f32[2,128,128]{2,1,0:T(8,128)S(1)}, f32[2,128,128]{2,1,0:T(8,128)S(1)}) custom-call(f32[128,128]{1,0:T(8,128)S(1)} %get-tuple-element.15.own_ref, f32[128,128]{1,0:T(8,128)S(1)} %collective-permute-done.1.partner_ref, f32[128,128]{1,0:T(8,128)S(1)} %get-tuple-element.14.cross_ref), custom_call_target="tpu_custom_call" | custom-call | flops 4294967296 | bytes 1048576 | tf_op jit(solution)/shard_map/pallas_call | solution.py:240
  12.0 2.2 %collective-permute-start.2 = (f32[2,128,128]{2,1,0:T(8,128)S(1)}, f32[2,128,128]{2,1,0:T(8,128)S(1)}, u32[]{:S(2)}, u32[]{:S(2)}) collective-permute-start(f32[2,128,128]{2,1,0:T(8,128)S(1)} %get-tuple-element.9.refs_0_), channel_id=1, source_target_pairs={{0,8},{4,12},{8,0},{12,4},{16,24},{20,28},{24,16},{28,20},{1,9},{5... | collective-permute-start | bytes 393224 | tf_op jit(solution)/shard_map/ppermute | solution.py:250
  14.2 0.0 collective-permute-start.3
  14.2 0.0 copy-start
  14.2 3.7 %shard_map.31.second_ref.refs_0_ = f32[2,128,128]{2,1,0:T(8,128)S(1)} custom-call(f32[2,128,128]{2,1,0:T(8,128)S(1)} %get-tuple-element.8.block_ref), custom_call_target="tpu_custom_call" | custom-call | flops 4294967296 | bytes 1048576 | tf_op jit(solution)/shard_map/pallas_call | solution.py:240
  18.0 0.0 collective-permute-done.2.refs_1_
  18.0 0.6 %collective-permute-start.4 = (f32[2,128,128]{2,1,0:T(8,128)S(1)}, f32[2,128,128]{2,1,0:T(8,128)S(1)}, u32[]{:S(2)}, u32[]{:S(2)}) collective-permute-start(f32[2,128,128]{2,1,0:T(8,128)S(1)} %collective-permute-done.2.refs_1_), channel_id=1, source_target_pairs={{0,4},{4,0},{8,12},{12,8},{16,20},{20,16},{24,28},{28,24},{1,5},{5... | collective-permute-start | bytes 393224 | tf_op jit(solution)/shard_map/ppermute | solution.py:250
  18.5 0.7 %collective-permute-start.5 = (f32[2,128,128]{2,1,0:T(8,128)S(1)}, f32[2,128,128]{2,1,0:T(8,128)S(1)}, u32[]{:S(2)}, u32[]{:S(2)}) collective-permute-start(f32[2,128,128]{2,1,0:T(8,128)S(1)} %shard_map.31.second_ref.refs_0_), channel_id=1, source_target_pairs={{0,8},{4,12},{8,0},{12,4},{16,24},{20,28},{24,16},{28,20},{1,9},{5... | collective-permute-start | bytes 393224 | tf_op jit(solution)/shard_map/ppermute | solution.py:250
  19.2 0.2 collective-permute-start.6
  19.4 0.0 collective-permute-done.3.refs_2_
  19.4 0.1 collective-permute-done.4.refs_3_
  19.5 0.0 collective-permute-done.moved_ref
  19.5 0.0 copy-done
  19.5 2.2 %shard_map.32 = (f32[1024,128]{1,0:T(8,128)S(1)}, f32[1024,128]{1,0:T(8,128)}) custom-call(f32[1024,128]{1,0:T(8,128)S(1)} %copy-done, f32[1024,128]{1,0:T(8,128)S(1)} %collective-permute-done.moved_ref, f32[2,128,128]{2,1,0:T(8,128)S(1)} %shard_map.31.second_ref.refs_0_, f32[2,128,128]{2,1,0:T(8,128)S(1)} %get-tuple-element.9.refs_0_, ...), custom_call_target="tpu_custom_call" | custom-call | flops 1048576 | bytes 1048576 | tf_op jit(solution)/shard_map/pallas_call | solution.py:240
  21.7 2.3 %collective-permute-done.5.refs_1_ = f32[2,128,128]{2,1,0:T(8,128)S(1)} collective-permute-done((f32[2,128,128]{2,1,0:T(8,128)S(1)}, f32[2,128,128]{2,1,0:T(8,128)S(1)}, u32[]{:S(2)}, u32[]{:S(2)}) %collective-permute-start.5) | collective-permute-done | bytes 131104 | tf_op jit(solution)/shard_map/ppermute | solution.py:250
  24.0 0.0 collective-permute-start.7
  24.0 0.0 collective-permute-done.6.refs_2_
  24.0 1.3 %collective-permute-done.7.refs_3_ = f32[2,128,128]{2,1,0:T(8,128)S(1)} collective-permute-done((f32[2,128,128]{2,1,0:T(8,128)S(1)}, f32[2,128,128]{2,1,0:T(8,128)S(1)}, u32[]{:S(2)}, u32[]{:S(2)}) %collective-permute-start.7) | collective-permute-done | bytes 131104 | tf_op jit(solution)/shard_map/ppermute | solution.py:250
  25.4 1.1 %shard_map.33 = f32[1024,128]{1,0:T(8,128)} custom-call(f32[1024,128]{1,0:T(8,128)S(1)} %get-tuple-element.11.mixed_ref, f32[2,128,128]{2,1,0:T(8,128)S(1)} %shard_map.31.second_ref.refs_0_, f32[2,128,128]{2,1,0:T(8,128)S(1)} %collective-permute-done.5.refs_1_, f32[2,128,128]{2,1,0:T(8,128)S(1)} %collective-permute-done.6.refs_2_, ...), custom_call_target="tpu_custom_call" | custom-call | flops 1048576 | bytes 1048576 | tf_op jit(solution)/shard_map/pallas_call | solution.py:240
Async XLA Ops:
  1.5 5.5 %collective-permute-start.1 = (f32[128,128]{1,0:T(8,128)S(1)}, f32[128,128]{1,0:T(8,128)S(1)}, u32[]{:S(2)}, u32[]{:S(2)}) collective-permute-start(f32[128,128]{1,0:T(8,128)S(1)} %get-tuple-element.15.own_ref), channel_id=1, source_target_pairs={{0,16},{4,20},{8,24},{12,28},{16,0},{20,4},{24,8},{28,12},{1,17},{... | collective-permute-start | bytes 196616 | tf_op jit(solution)/shard_map/ppermute | solution.py:250
  4.6 15.0 %collective-permute-start = (f32[1024,128]{1,0:T(8,128)}, f32[1024,128]{1,0:T(8,128)S(1)}, u32[]{:S(2)}, u32[]{:S(2)}) collective-permute-start(f32[1024,128]{1,0:T(8,128)} %factor_ref.1), channel_id=1, source_target_pairs={{0,16},{4,20},{8,24},{12,28},{16,0},{20,4},{24,8},{28,12},{1,17},{... | collective-permute-start | bytes 1572872 | tf_op jit(solution)/shard_map/ppermute | solution.py:250
  12.0 5.9 %collective-permute-start.2 = (f32[2,128,128]{2,1,0:T(8,128)S(1)}, f32[2,128,128]{2,1,0:T(8,128)S(1)}, u32[]{:S(2)}, u32[]{:S(2)}) collective-permute-start(f32[2,128,128]{2,1,0:T(8,128)S(1)} %get-tuple-element.9.refs_0_), channel_id=1, source_target_pairs={{0,8},{4,12},{8,0},{12,4},{16,24},{20,28},{24,16},{28,20},{1,9},{5... | collective-permute-start | bytes 393224 | tf_op jit(solution)/shard_map/ppermute | solution.py:250
  14.2 5.2 %collective-permute-start.3 = (f32[2,128,128]{2,1,0:T(8,128)S(1)}, f32[2,128,128]{2,1,0:T(8,128)S(1)}, u32[]{:S(2)}, u32[]{:S(2)}) collective-permute-start(f32[2,128,128]{2,1,0:T(8,128)S(1)} %get-tuple-element.9.refs_0_), channel_id=1, source_target_pairs={{0,4},{4,0},{8,12},{12,8},{16,20},{20,16},{24,28},{28,24},{1,5},{5... | collective-permute-start | bytes 393224 | tf_op jit(solution)/shard_map/ppermute | solution.py:250
  14.2 5.3 %copy-start = (f32[1024,128]{1,0:T(8,128)S(1)}, f32[1024,128]{1,0:T(8,128)}, u32[]{:S(2)}) copy-start(f32[1024,128]{1,0:T(8,128)} %factor_ref.1) | copy-start | bytes 1572868
  18.0 1.6 %collective-permute-start.4 = (f32[2,128,128]{2,1,0:T(8,128)S(1)}, f32[2,128,128]{2,1,0:T(8,128)S(1)}, u32[]{:S(2)}, u32[]{:S(2)}) collective-permute-start(f32[2,128,128]{2,1,0:T(8,128)S(1)} %collective-permute-done.2.refs_1_), channel_id=1, source_target_pairs={{0,4},{4,0},{8,12},{12,8},{16,20},{20,16},{24,28},{28,24},{1,5},{5... | collective-permute-start | bytes 393224 | tf_op jit(solution)/shard_map/ppermute | solution.py:250
  18.5 5.5 %collective-permute-start.5 = (f32[2,128,128]{2,1,0:T(8,128)S(1)}, f32[2,128,128]{2,1,0:T(8,128)S(1)}, u32[]{:S(2)}, u32[]{:S(2)}) collective-permute-start(f32[2,128,128]{2,1,0:T(8,128)S(1)} %shard_map.31.second_ref.refs_0_), channel_id=1, source_target_pairs={{0,8},{4,12},{8,0},{12,4},{16,24},{20,28},{24,16},{28,20},{1,9},{5... | collective-permute-start | bytes 393224 | tf_op jit(solution)/shard_map/ppermute | solution.py:250
  19.2 4.8 %collective-permute-start.6 = (f32[2,128,128]{2,1,0:T(8,128)S(1)}, f32[2,128,128]{2,1,0:T(8,128)S(1)}, u32[]{:S(2)}, u32[]{:S(2)}) collective-permute-start(f32[2,128,128]{2,1,0:T(8,128)S(1)} %shard_map.31.second_ref.refs_0_), channel_id=1, source_target_pairs={{0,4},{4,0},{8,12},{12,8},{16,20},{20,16},{24,28},{28,24},{1,5},{5... | collective-permute-start | bytes 393224 | tf_op jit(solution)/shard_map/ppermute | solution.py:250
  24.0 1.3 %collective-permute-start.7 = (f32[2,128,128]{2,1,0:T(8,128)S(1)}, f32[2,128,128]{2,1,0:T(8,128)S(1)}, u32[]{:S(2)}, u32[]{:S(2)}) collective-permute-start(f32[2,128,128]{2,1,0:T(8,128)S(1)} %collective-permute-done.5.refs_1_), channel_id=1, source_target_pairs={{0,4},{4,0},{8,12},{12,8},{16,20},{20,16},{24,28},{28,24},{1,5},{5... | collective-permute-start | bytes 393224 | tf_op jit(solution)/shard_map/ppermute | solution.py:250

commit v3 on v2

v3 whole, which is shorter than its diff:
```python
import functools
import jax
import jax.numpy as jnp
from jax import lax
from jax.experimental import pallas as pl
from jax.experimental.pallas import tpu as pltpu
from jax.sharding import PartitionSpec as P

SWEEPS = 3
FLOOR = 0.01
TOLERANCE = 3e-6


def schedule(bound, steps=None, weight=1.0, goal=1e-6):
    theta = bound / (2.0 + bound)
    mus = []
    while len(mus) < steps if steps else theta > goal:
        mus.append(2.0 / (2.0 - theta * theta))
        theta = theta * theta / (2.0 - theta * theta)
    return 1.0 / (1.0 + 0.5 * bound), tuple(mus), weight


def split(x):
    high = x.astype(jnp.bfloat16)
    x = x - high.astype(jnp.float32)
    middle = x.astype(jnp.bfloat16)
    return high, middle, (x - middle.astype(jnp.float32)).astype(jnp.bfloat16)


def product(a, b):
    n = b.shape[1]
    a_high, a_middle, a_low = split(a)
    b_high, b_middle, b_low = split(b)
    wide = jnp.concatenate([b_high, b_middle], axis=1)
    most = jnp.dot(
        jnp.concatenate([a_high, a_middle], axis=1),
        jnp.concatenate([wide, wide], axis=0),
        preferred_element_type=jnp.float32,
    )
    rest = jnp.dot(
        jnp.concatenate([a_high, a_low], axis=1),
        jnp.concatenate([b_low, b_high], axis=0),
        preferred_element_type=jnp.float32,
    )
    return most[:, :n] + (most[:, n:] + rest)


def exact(a, b):
    return jnp.dot(a, b, precision=lax.Precision.HIGHEST, preferred_element_type=jnp.float32)


def identity_of(n):
    row = lax.broadcasted_iota(jnp.int32, (n, n), 0)
    col = lax.broadcasted_iota(jnp.int32, (n, n), 1)
    return (row == col).astype(jnp.float32)


def ratios_of(m, eye):
    kept = m * eye
    spread = jnp.sum(kept, axis=0, keepdims=True) - jnp.sum(kept, axis=1, keepdims=True)
    return m * spread / (spread * spread + 2.0 * m * m + FLOOR)


def sure_sweep(m, qt, eye):
    n = m.shape[0]
    ratios = ratios_of(m, eye)
    a = 0.25 * (ratios - ratios.T)
    system = eye - exact(a, a)
    scale, mus, _ = schedule(n * n / 32.0)

    def newton(_, y):
        return y + exact(y, eye - exact(system, y))

    y = lax.fori_loop(0, len(mus) + 6, newton, scale * eye)
    x = exact(y, eye + a)
    x = x + exact(x, eye - (x - exact(a, x)))
    turn = 2.0 * x - eye
    return exact(turn.T, exact(m, turn)), exact(turn.T, qt)


def solve(blocks, plans, eye, keep):
    n = eye.shape[0]
    some = range(len(blocks))
    ms, qts = list(blocks), None
    worst = jnp.zeros((1, n), jnp.float32)
    for index, (scale, mus, weight) in enumerate(plans):
        carried = keep or index + 1 < len(plans)
        skews = [0.5 * ratios_of(m, eye) for m in ms]
        if carried:
            firsts = [product(jnp.concatenate([a, m], axis=0), a) for a, m in zip(skews, ms)]
        else:
            firsts = [product(a, a) for a in skews]
        errors = [(1.0 - scale) * eye + scale * first[:n] for first in firsts]
        stacks = [scale * (eye - a) for a in skews]
        if carried:
            stacks = [
                jnp.concatenate([stack, scale * (m + first[n:])], axis=0)
                for stack, m, first in zip(stacks, ms, firsts)
            ]
        for mu in mus:
            steps = [
                product(jnp.concatenate([error, stack], axis=0), error)
                for error, stack in zip(errors, stacks)
            ]
            errors = [(1.0 - mu) * eye + mu * step[:n] for step in steps]
            stacks = [mu * (stack + step[n:]) for stack, step in zip(stacks, steps)]
        for error in errors:
            worst = worst + weight * jnp.sum(error * error, axis=0, keepdims=True)
        backs = [2.0 * stack[:n] - eye for stack in stacks]
        rights = [[] for _ in some]
        if carried:
            rights = [[2.0 * stack[n:] - m] for stack, m in zip(stacks, ms)]
        if qts is not None:
            rights = [right + [qt] for right, qt in zip(rights, qts)]
        turned = [
            product(back, jnp.concatenate(right, axis=1)) for back, right in zip(backs, rights)
        ]
        qts = backs if qts is None else [both[:, -n:] for both in turned]
        if carried:
            ms = [both[:, :n] for both in turned]
    return ms, qts, worst


def settled(worst):
    return jnp.sum(worst) <= TOLERANCE * TOLERANCE * worst.shape[1]


def solve_surely(blocks, m_ref, qt_ref, eye):
    for k in range(len(blocks)):
        m_ref[k] = blocks[k]
        qt_ref[k] = eye

    def again(step, carry):
        k = step // SWEEPS
        m_ref[k], qt_ref[k] = sure_sweep(m_ref[k], qt_ref[k], eye)
        return carry

    lax.fori_loop(0, SWEEPS * len(blocks), again, 0)


PLANS = (
    (schedule(4.0, 4), schedule(3.0, 4), schedule(0.95, 3)),
    (schedule(0.8, 3), schedule(0.5, 3), schedule(0.2, 2, 0.01)),
)


def halves(x):
    high = x.astype(jnp.bfloat16)
    return high, (x - high.astype(jnp.float32)).astype(jnp.bfloat16)


def quick(a, b):
    n = b.shape[1]
    wide = jnp.concatenate(halves(b), axis=1)
    both = jnp.dot(
        jnp.concatenate(halves(a), axis=1),
        jnp.concatenate([wide, wide], axis=0),
        preferred_element_type=jnp.float32,
    )
    return both[:, :n] + both[:, n:]


def pair_up(first, last, cross):
    n = first.shape[0]
    row = lax.broadcasted_iota(jnp.int32, (n, n), 0) < n // 2
    col = lax.broadcasted_iota(jnp.int32, (n, n), 1) < n // 2
    corner = jnp.where(jnp.logical_and(jnp.logical_not(row), col), cross, 0.0)
    return jnp.where(row == col, jnp.where(row, first, last), corner + corner.T)


def rows_of(pair, n):
    return pl.ds(pl.multiple_of(pair * n, n), n)


def first_kernel(own_ref, packed_ref, qt_ref, m_ref):
    n = own_ref.shape[0]
    half = n // 2
    eye = identity_of(n)
    col = lax.broadcasted_iota(jnp.int32, (half, n), 1) < half

    def finish(m, qt):
        packed_ref[:n, :] = qt
        packed_ref[n:, :] = jnp.where(col, m[:half], m[half:])

    (m,), (qt,), worst = solve([own_ref[...]], PLANS[0], eye, True)
    qt_ref[0] = qt
    m_ref[0] = m
    finish(m, qt)

    @pl.when(jnp.logical_not(settled(worst)))
    def _():
        solve_surely([own_ref[...]], m_ref, qt_ref, eye)
        finish(m_ref[0], qt_ref[0])


def columns_kernel(factor_ref, cross_ref, qt_ref, columns_ref, right_ref, moved_ref):
    order_size, n = factor_ref.shape
    half, middle = n // 2, order_size // 2
    turn = qt_ref[0].T
    moved_ref[...] = product(cross_ref[...], turn)
    for start in range(0, middle, n):
        upper = quick(factor_ref[start : start + n, :], turn)
        lower = quick(factor_ref[middle + start : middle + start + n, :], turn)
        columns_ref[start : start + n, :] = upper
        columns_ref[middle + start : middle + start + n, :] = lower
        right_ref[start : start + n, :] = jnp.concatenate([upper[:, half:], lower[:, half:]], axis=1)


def second_kernel(packed_ref, m_in_ref, own_ref, moved_ref, second_ref, first_ref, block_ref, m_ref):
    n = moved_ref.shape[0]
    eye = identity_of(n)
    qt, packed = packed_ref[:n, :], packed_ref[n:, :]
    first_ref[0] = own_ref[0]
    first_ref[1] = qt
    cross = product(qt, moved_ref[...])
    own, partner = m_in_ref[0], jnp.concatenate([packed, packed], axis=0)
    blocks = [pair_up(own, partner, cross), pair_up(partner, own, cross.T)]
    block_ref[0], block_ref[1] = blocks
    _, (second_ref[0], second_ref[1]), worst = solve(blocks, PLANS[1], eye, False)

    @pl.when(jnp.logical_not(settled(worst)))
    def _():
        solve_surely([block_ref[0], block_ref[1]], m_ref, second_ref, eye)


def turn_kernel(far, columns_ref, right_ref, second_ref, first_ref, mixed_ref, out_ref):
    order_size, n = columns_ref.shape
    half, middle = n // 2, order_size // 2
    me = lax.axis_index("wide")
    row = lax.broadcasted_iota(jnp.int32, (n, n), 0) < half
    turn = second_ref[0].T
    out_ref[...] = jnp.zeros_like(out_ref)
    out_ref[rows_of(me, n), :] = quick(jnp.where(row, first_ref[0], 0.0).T, turn)
    out_ref[rows_of(me ^ far, n), :] = quick(jnp.where(row, 0.0, first_ref[1]).T, turn)
    for start in range(0, middle, n):
        upper, lower = slice(start, start + n), slice(middle + start, middle + start + n)
        right = right_ref[upper, :]
        left = columns_ref[upper, :]
        mixed_ref[upper, :] = quick(jnp.concatenate([left[:, :half], right[:, :half]], axis=1), turn)
        left = columns_ref[lower, :]
        mixed_ref[lower, :] = quick(jnp.concatenate([left[:, :half], right[:, half:]], axis=1), turn)


def trade_kernel(masks, far, turned_ref, *refs):
    refs, mixed_ref = refs[:-1], refs[-1]
    n = turned_ref.shape[1]
    half = n // 2
    me = lax.axis_index("wide")
    for mask, (near_ref, away_ref) in zip(masks, two_by_two(refs)):
        pair, other = rows_of(me ^ mask, n), rows_of(me ^ mask ^ far, n)
        near = quick(near_ref[...], turned_ref[pair, :])
        away = quick(away_ref[...], turned_ref[other, :])
        mixed_ref[pair, :] = jnp.concatenate([near[:half], away[half:]], axis=0)
        mixed_ref[other, :] = jnp.concatenate([away[:half], near[half:]], axis=0)


def two_by_two(refs):
    couples, held = [], []
    for ref in refs:
        held += [ref.at[side] for side in range(ref.shape[0])]
        if len(held) == 2:
            couples.append(held)
            held = []
    return couples


def rows_kernel(masks, far, mixed_ref, *refs):
    refs, out_ref = refs[:-1], refs[-1]
    n = mixed_ref.shape[1]
    me = lax.axis_index("wide")
    for mask, turn_ref in zip(masks, refs):
        for side in range(2):
            rows = rows_of(me ^ mask ^ (far * side), n)
            out_ref[rows, :] = quick(turn_ref[side], mixed_ref[rows, :])


def last_rows_kernel(masks, far, mixed_ref, *refs):
    turn_refs, (_, out_ref, block_ref, sem_ref) = refs[:-4], refs[-4:]
    n = mixed_ref.shape[1]
    me = lax.axis_index("wide")
    copies = []
    for mask, turn_ref in zip(masks, turn_refs):
        for side in range(2):
            rows = rows_of(me ^ mask ^ (far * side), n)
            place = len(copies)
            block_ref[place] = quick(turn_ref[side], mixed_ref[rows, :])
            copy = pltpu.make_async_copy(block_ref.at[place], out_ref.at[rows, :], sem_ref.at[place])
            copy.start()
            copies.append(copy)
    for copy in copies:
        copy.wait()


def call(kernel, out_shape, scratch_shapes, flops, *args, **more):
    return pl.pallas_call(
        kernel,
        out_shape=out_shape,
        scratch_shapes=scratch_shapes,
        compiler_params=pltpu.CompilerParams(vmem_limit_bytes=48 * 1024 * 1024),
        cost_estimate=pl.CostEstimate(flops=flops, bytes_accessed=2**20, transcendentals=0),
        **more,
    )(*args)


def swap(shard, mask):
    return lax.ppermute(shard, "wide", [(i, i ^ mask) for i in range(lax.axis_size("wide"))])


def after(value, gate):
    return lax.optimization_barrier((value, gate))[0]


def spread_first(own, early, both, far, gate):
    pieces = [(0, (both,))]
    if early:
        pieces.append((far // 2, early))
    bit = far // 4
    while bit:
        pieces += [
            (mask | bit, tuple(swap(after(held, gate), bit) for held in couple))
            for mask, couple in pieces
        ]
        bit //= 2
    return [mask for mask, _ in pieces], [held for _, couple in pieces for held in couple]


def spread_second(both, far, gate):
    pieces = [(0, both)]
    bit = far // 2
    while bit:
        pieces += [
            (mask | bit, swap(after(held, gate) if mask and bit == 1 else held, bit))
            for mask, held in pieces
        ]
        bit //= 2
    return pieces


def body(factor):
    far = lax.axis_size("wide") // 2
    me = lax.axis_index("wide")
    order_size, n = factor.shape

    def like(*shape):
        return jax.ShapeDtypeStruct(shape, jnp.float32)

    one, two, tall = like(1, n, n), like(2, n, n), like(order_size, n)
    own = lax.dynamic_slice_in_dim(factor, me * n, n, 0)
    cross = lax.dynamic_slice_in_dim(factor, (me ^ far) * n, n, 0)
    packed, qt, m = call(first_kernel, (like(n + n // 2, n), one, one), [], 2**32, own)
    packed = swap(packed, far)
    columns, right, moved = call(
        columns_kernel, (tall, like(order_size // 2, n), like(n, n)), [], 2**28, factor, cross, qt
    )
    right = swap(right, far)
    mine = after(qt, moved)
    early = (swap(mine, far // 2), swap(mine, far // 2 | far)) if far > 1 else ()
    scratch = [pltpu.VMEM((2, n, n), jnp.float32)] * 2
    second, both = call(second_kernel, (two, two), scratch, 2**31, packed, m, qt, moved)
    masks, firsts = spread_first(qt, early, both, far, second)
    turned, eigen_basis = call(
        functools.partial(turn_kernel, far), (tall, tall), [], 2**31, columns, right, second, both
    )
    mixed = call(functools.partial(trade_kernel, masks, far), tall, [], 2**31, turned, *firsts)
    pieces = spread_second(second, far, mixed)
    soon = [piece for piece in pieces if piece[0] < 2 or not piece[0] & 1]
    late = [piece for piece in pieces if piece[0] >= 2 and piece[0] & 1]
    masks, held = zip(*soon)
    rotated = call(functools.partial(rows_kernel, masks, far), tall, [], 2**29, mixed, *held)
    if late:
        masks, held = zip(*late)
        anywhere = pl.BlockSpec(memory_space=pl.ANY)
        inside = pl.BlockSpec(memory_space=pltpu.VMEM)
        rotated = call(
            functools.partial(last_rows_kernel, masks, far),
            tall,
            [
                pltpu.VMEM((2 * len(late), n, n), jnp.float32),
                pltpu.SemaphoreType.DMA((2 * len(late),)),
            ],
            2**29,
            mixed,
            *held,
            rotated,
            in_specs=[inside] * (1 + len(late)) + [anywhere],
            out_specs=anywhere,
            input_output_aliases={1 + len(late): 0},
        )
    return (rotated, eigen_basis)


def solution(mesh):
    return jax.shard_map(
        body,
        mesh=mesh,
        in_specs=(P("layer", "wide"),),
        out_specs=(P("layer", "wide"), P("layer", "wide")),
        check_vma=False,
    )
```

time: 26.7 us -> 46.9 us (1.76)
  the two profiles are of different devices: /device:TPU:0 before, /device:TPU:21 now
where the time goes in v3:
time: 46.9 us; the launch traced here: 46.1 us
  starting transfers between devices  33 us (70%)
  Pallas kernels  11.4 us (24%)
  local copies, waits for them, and re-layouts  0.89 us (2%)
  between operations  0.69 us (1%)
    ppermute x10, starting transfers between devices, swap(): lax.ppermute(shard, 'wide', [(i, i ^ mask) for i in range(lax.axis_size('...  33 us
    pallas_call x7, Pallas kernels, call(): pl.pallas_call(kernel, out_shape=out_shape, scratch_shapes=scratch_shapes...  11.4 us
  transfers between devices with their start and end apart: 10, of which 0 were waited for; matrix products, arithmetic and copies ran while one was open for 0% of the time, Pallas kernels for 14%

profile of v3, /device:TPU:21, one launch (start us, length us, event | category | flops | bytes accessed | tf_op | source)
XLA Modules:
  0.0 46.1 jit_solution(8439597476136345918)
XLA Ops:
  0.6 0.9 %constant_dynamic-slice_fusion = (f32[128,128]{1,0:T(8,128)S(1)}, f32[128,128]{1,0:T(8,128)S(1)}) fusion(f32[1024,128]{1,0:T(8,128)} %factor_ref.1, s32[]{:T(128)S(6)} %select_n.7, s32[]{:T(128)S(6)} %select_n.6), kind=kLoop, calls=%fused_computation | loop fusion | bytes 262152 | tf_op jit(solution)/shard_map/dynamic_slice | solution.py:348
  1.5 0.0 copy-start
  1.5 4.0 %shard_map.30 = (f32[192,128]{1,0:T(8,128)S(1)}, f32[1,128,128]{2,1,0:T(8,128)S(1)}, f32[1,128,128]{2,1,0:T(8,128)S(1)}) custom-call(f32[128,128]{1,0:T(8,128)S(1)} %get-tuple-element.32.own_ref), custom_call_target="tpu_custom_call" | custom-call | flops 4294967296 | bytes 1048576 | tf_op jit(solution)/shard_map/pallas_call | solution.py:295
  5.5 0.3 collective-permute-start.1
  5.8 0.0 copy-done
  5.8 0.5 %shard_map.31 = (f32[1024,128]{1,0:T(8,128)S(1)}, f32[512,128]{1,0:T(8,128)S(1)}, f32[128,128]{1,0:T(8,128)S(1)}) custom-call(f32[1024,128]{1,0:T(8,128)S(1)} %copy-done, f32[128,128]{1,0:T(8,128)S(1)} %get-tuple-element.33.cross_ref, f32[1,128,128]{2,1,0:T(8,128)S(1)} %get-tuple-element.26.qt_ref.own_ref), custom_call_target="tpu_custom_call" | custom-call | flops 268435456 | bytes 1048576 | tf_op jit(solution)/shard_map/pallas_call | solution.py:295
  6.3 1.3 %collective-permute-start = (f32[512,128]{1,0:T(8,128)S(1)}, f32[512,128]{1,0:T(8,128)S(1)}, u32[]{:S(2)}, u32[]{:S(2)}) collective-permute-start(f32[512,128]{1,0:T(8,128)S(1)} %get-tuple-element.19), channel_id=1, source_target_pairs={{0,16},{4,20},{8,24},{12,28},{16,0},{20,4},{24,8},{28,12},{1,17},{... | collective-permute-start | bytes 786440 | tf_op jit(solution)/shard_map/ppermute | solution.py:306
  7.6 23.6 %collective-permute-start.2 = (f32[1,128,128]{2,1,0:T(8,128)S(1)}, f32[1,128,128]{2,1,0:T(8,128)S(1)}, u32[]{:S(2)}, u32[]{:S(2)}) collective-permute-start(f32[1,128,128]{2,1,0:T(8,128)S(1)} %get-tuple-element.26.qt_ref.own_ref), channel_id=1, source_target_pairs={{0,8},{4,12},{8,0},{12,4},{16,24},{20,28},{24,16},{28,20},{1,9},{5... | collective-permute-start | bytes 196616 | tf_op jit(solution)/shard_map/ppermute | solution.py:306
  31.2 1.1 %collective-permute-start.3 = (f32[1,128,128]{2,1,0:T(8,128)S(1)}, f32[1,128,128]{2,1,0:T(8,128)S(1)}, u32[]{:S(2)}, u32[]{:S(2)}) collective-permute-start(f32[1,128,128]{2,1,0:T(8,128)S(1)} %get-tuple-element.26.qt_ref.own_ref), channel_id=1, source_target_pairs={{0,24},{4,28},{8,16},{12,20},{16,8},{20,12},{24,0},{28,4},{1,25},{... | collective-permute-start | bytes 196616 | tf_op jit(solution)/shard_map/ppermute | solution.py:306
  32.3 0.0 collective-permute-done.1.packed_ref
  32.3 3.6 %shard_map.32 = (f32[2,128,128]{2,1,0:T(8,128)S(1)}, f32[2,128,128]{2,1,0:T(8,128)S(1)}) custom-call(f32[192,128]{1,0:T(8,128)S(1)} %collective-permute-done.1.packed_ref, f32[1,128,128]{2,1,0:T(8,128)S(1)} %get-tuple-element.21.m_in_ref, f32[1,128,128]{2,1,0:T(8,128)S(1)} %get-tuple-element.26.qt_ref.own_ref, f32[128,128]{1,0:T(8,128)S(1)} %get-tuple-element.22.moved_ref), custom_call_target="tpu_custom_call" | custom-call | flops 2147483648 | bytes 1048576 | tf_op jit(solution)/shard_map/pallas_call | solution.py:295
  35.9 1.5 %collective-permute-start.7 = (f32[2,128,128]{2,1,0:T(8,128)S(1)}, f32[2,128,128]{2,1,0:T(8,128)S(1)}, u32[]{:S(2)}, u32[]{:S(2)}) collective-permute-start(f32[2,128,128]{2,1,0:T(8,128)S(1)} %get-tuple-element.23.second_ref.refs_0_), channel_id=1, source_target_pairs={{0,8},{4,12},{8,0},{12,4},{16,24},{20,28},{24,16},{28,20},{1,9},{5... | collective-permute-start | bytes 393224 | tf_op jit(solution)/shard_map/ppermute | solution.py:306
  37.4 3.8 %collective-permute-start.9 = (f32[2,128,128]{2,1,0:T(8,128)S(1)}, f32[2,128,128]{2,1,0:T(8,128)S(1)}, u32[]{:S(2)}, u32[]{:S(2)}) collective-permute-start(f32[2,128,128]{2,1,0:T(8,128)S(1)} %get-tuple-element.23.second_ref.refs_0_), channel_id=1, source_target_pairs={{0,4},{4,0},{8,12},{12,8},{16,20},{20,16},{24,28},{28,24},{1,5},{5... | collective-permute-start | bytes 393224 | tf_op jit(solution)/shard_map/ppermute | solution.py:306
  41.2 0.0 collective-permute-done.2.refs_1_
  41.2 0.0 collective-permute-start.4
  41.2 0.0 collective-permute-done.3.refs_2_
  41.2 0.5 %collective-permute-start.5 = (f32[1,128,128]{2,1,0:T(8,128)S(1)}, f32[1,128,128]{2,1,0:T(8,128)S(1)}, u32[]{:S(2)}, u32[]{:S(2)}) collective-permute-start(f32[1,128,128]{2,1,0:T(8,128)S(1)} %collective-permute-done.2.refs_1_), channel_id=1, source_target_pairs={{0,4},{4,0},{8,12},{12,8},{16,20},{20,16},{24,28},{28,24},{1,5},{5... | collective-permute-start | bytes 196616 | tf_op jit(solution)/shard_map/ppermute | solution.py:306
  41.7 0.0 collective-permute-done.right_ref
  41.7 0.1 collective-permute-start.6
  41.8 1.1 %shard_map.33 = (f32[1024,128]{1,0:T(8,128)S(1)}, f32[1024,128]{1,0:T(8,128)}) custom-call(f32[1024,128]{1,0:T(8,128)S(1)} %get-tuple-element.18.columns_ref, f32[512,128]{1,0:T(8,128)S(1)} %collective-permute-done.right_ref, f32[2,128,128]{2,1,0:T(8,128)S(1)} %get-tuple-element.23.second_ref.refs_0_, f32[2,128,128]{2,1,0:T(8,128)S(1)} %get-tuple-element.27.first_ref.refs_0_), custom_call_target="tpu_custom_call" | custom-call | flops 2147483648 | bytes 1048576 | tf_op jit(solution)/shard_map/pallas_call | solution.py:295
  42.9 0.0 collective-permute-done.5.refs_4_
  42.9 0.0 collective-permute-done.6.refs_5_
  43.0 0.0 collective-permute-done.4.refs_3_
  43.0 0.3 shard_map.34.mixed_ref
  43.3 0.0 collective-permute-done.7.refs_1_
  43.3 0.8 %collective-permute-start.8 = (f32[2,128,128]{2,1,0:T(8,128)S(1)}, f32[2,128,128]{2,1,0:T(8,128)S(1)}, u32[]{:S(2)}, u32[]{:S(2)}) collective-permute-start(f32[2,128,128]{2,1,0:T(8,128)S(1)} %collective-permute-done.7.refs_1_), channel_id=1, source_target_pairs={{0,4},{4,0},{8,12},{12,8},{16,20},{20,16},{24,28},{28,24},{1,5},{5... | collective-permute-start | bytes 393224 | tf_op jit(solution)/shard_map/ppermute | solution.py:306
  44.2 0.0 collective-permute-done.9.refs_2_
  44.2 1.1 %shard_map.35.refs_1_ = f32[1024,128]{1,0:T(8,128)} custom-call(f32[1024,128]{1,0:T(8,128)S(1)} %shard_map.34.mixed_ref, f32[2,128,128]{2,1,0:T(8,128)S(1)} %get-tuple-element.23.second_ref.refs_0_, f32[2,128,128]{2,1,0:T(8,128)S(1)} %collective-permute-done.7.refs_1_, f32[2,128,128]{2,1,0:T(8,128)S(1)} %collective-permute-done.9.refs_2_), custom_call_target="tpu_custom_call" | custom-call | flops 536870912 | bytes 1048576 | tf_op jit(solution)/shard_map/pallas_call | solution.py:295
  45.3 0.0 collective-permute-done.8.refs_0_
  45.3 0.9 %shard_map.36 = f32[1024,128]{1,0:T(8,128)} custom-call(f32[1024,128]{1,0:T(8,128)S(1)} %shard_map.34.mixed_ref, f32[2,128,128]{2,1,0:T(8,128)S(1)} %collective-permute-done.8.refs_0_, f32[1024,128]{1,0:T(8,128)} %shard_map.35.refs_1_), custom_call_target="tpu_custom_call", output_to_operand_aliasing={{}: (2, {})} | custom-call | flops 536870912 | bytes 1048576 | tf_op jit(solution)/shard_map/pallas_call | solution.py:295
Async XLA Ops:
  1.5 4.3 %copy-start = (f32[1024,128]{1,0:T(8,128)S(1)}, f32[1024,128]{1,0:T(8,128)}, u32[]{:S(2)}) copy-start(f32[1024,128]{1,0:T(8,128)} %factor_ref.1) | copy-start | bytes 1572868
  5.5 26.8 %collective-permute-start.1 = (f32[192,128]{1,0:T(8,128)S(1)}, f32[192,128]{1,0:T(8,128)S(1)}, u32[]{:S(2)}, u32[]{:S(2)}) collective-permute-start(f32[192,128]{1,0:T(8,128)S(1)} %get-tuple-element.20), channel_id=1, source_target_pairs={{0,16},{4,20},{8,24},{12,28},{16,0},{20,4},{24,8},{28,12},{1,17},{... | collective-permute-start | bytes 294920 | tf_op jit(solution)/shard_map/ppermute | solution.py:306
  6.3 35.4 %collective-permute-start = (f32[512,128]{1,0:T(8,128)S(1)}, f32[512,128]{1,0:T(8,128)S(1)}, u32[]{:S(2)}, u32[]{:S(2)}) collective-permute-start(f32[512,128]{1,0:T(8,128)S(1)} %get-tuple-element.19), channel_id=1, source_target_pairs={{0,16},{4,20},{8,24},{12,28},{16,0},{20,4},{24,8},{28,12},{1,17},{... | collective-permute-start | bytes 786440 | tf_op jit(solution)/shard_map/ppermute | solution.py:306
  7.6 33.6 %collective-permute-start.2 = (f32[1,128,128]{2,1,0:T(8,128)S(1)}, f32[1,128,128]{2,1,0:T(8,128)S(1)}, u32[]{:S(2)}, u32[]{:S(2)}) collective-permute-start(f32[1,128,128]{2,1,0:T(8,128)S(1)} %get-tuple-element.26.qt_ref.own_ref), channel_id=1, source_target_pairs={{0,8},{4,12},{8,0},{12,4},{16,24},{20,28},{24,16},{28,20},{1,9},{5... | collective-permute-start | bytes 196616 | tf_op jit(solution)/shard_map/ppermute | solution.py:306
  31.2 10.0 %collective-permute-start.3 = (f32[1,128,128]{2,1,0:T(8,128)S(1)}, f32[1,128,128]{2,1,0:T(8,128)S(1)}, u32[]{:S(2)}, u32[]{:S(2)}) collective-permute-start(f32[1,128,128]{2,1,0:T(8,128)S(1)} %get-tuple-element.26.qt_ref.own_ref), channel_id=1, source_target_pairs={{0,24},{4,28},{8,16},{12,20},{16,8},{20,12},{24,0},{28,4},{1,25},{... | collective-permute-start | bytes 196616 | tf_op jit(solution)/shard_map/ppermute | solution.py:306
  35.9 7.5 %collective-permute-start.7 = (f32[2,128,128]{2,1,0:T(8,128)S(1)}, f32[2,128,128]{2,1,0:T(8,128)S(1)}, u32[]{:S(2)}, u32[]{:S(2)}) collective-permute-start(f32[2,128,128]{2,1,0:T(8,128)S(1)} %get-tuple-element.23.second_ref.refs_0_), channel_id=1, source_target_pairs={{0,8},{4,12},{8,0},{12,4},{16,24},{20,28},{24,16},{28,20},{1,9},{5... | collective-permute-start | bytes 393224 | tf_op jit(solution)/shard_map/ppermute | solution.py:306
  37.4 6.8 %collective-permute-start.9 = (f32[2,128,128]{2,1,0:T(8,128)S(1)}, f32[2,128,128]{2,1,0:T(8,128)S(1)}, u32[]{:S(2)}, u32[]{:S(2)}) collective-permute-start(f32[2,128,128]{2,1,0:T(8,128)S(1)} %get-tuple-element.23.second_ref.refs_0_), channel_id=1, source_target_pairs={{0,4},{4,0},{8,12},{12,8},{16,20},{20,16},{24,28},{28,24},{1,5},{5... | collective-permute-start | bytes 393224 | tf_op jit(solution)/shard_map/ppermute | solution.py:306
  41.2 1.8 %collective-permute-start.4 = (f32[2,128,128]{2,1,0:T(8,128)S(1)}, f32[2,128,128]{2,1,0:T(8,128)S(1)}, u32[]{:S(2)}, u32[]{:S(2)}) collective-permute-start(f32[2,128,128]{2,1,0:T(8,128)S(1)} %get-tuple-element.27.first_ref.refs_0_), channel_id=1, source_target_pairs={{0,4},{4,0},{8,12},{12,8},{16,20},{20,16},{24,28},{28,24},{1,5},{5... | collective-permute-start | bytes 393224 | tf_op jit(solution)/shard_map/ppermute | solution.py:306
  41.2 1.7 %collective-permute-start.5 = (f32[1,128,128]{2,1,0:T(8,128)S(1)}, f32[1,128,128]{2,1,0:T(8,128)S(1)}, u32[]{:S(2)}, u32[]{:S(2)}) collective-permute-start(f32[1,128,128]{2,1,0:T(8,128)S(1)} %collective-permute-done.2.refs_1_), channel_id=1, source_target_pairs={{0,4},{4,0},{8,12},{12,8},{16,20},{20,16},{24,28},{28,24},{1,5},{5... | collective-permute-start | bytes 196616 | tf_op jit(solution)/shard_map/ppermute | solution.py:306
  41.7 1.3 %collective-permute-start.6 = (f32[1,128,128]{2,1,0:T(8,128)S(1)}, f32[1,128,128]{2,1,0:T(8,128)S(1)}, u32[]{:S(2)}, u32[]{:S(2)}) collective-permute-start(f32[1,128,128]{2,1,0:T(8,128)S(1)} %collective-permute-done.3.refs_2_), channel_id=1, source_target_pairs={{0,4},{4,0},{8,12},{12,8},{16,20},{20,16},{24,28},{28,24},{1,5},{5... | collective-permute-start | bytes 196616 | tf_op jit(solution)/shard_map/ppermute | solution.py:306
  43.3 1.9 %collective-permute-start.8 = (f32[2,128,128]{2,1,0:T(8,128)S(1)}, f32[2,128,128]{2,1,0:T(8,128)S(1)}, u32[]{:S(2)}, u32[]{:S(2)}) collective-permute-start(f32[2,128,128]{2,1,0:T(8,128)S(1)} %collective-permute-done.7.refs_1_), channel_id=1, source_target_pairs={{0,4},{4,0},{8,12},{12,8},{16,20},{20,16},{24,28},{28,24},{1,5},{5... | collective-permute-start | bytes 393224 | tf_op jit(solution)/shard_map/ppermute | solution.py:306
